TPU v7x, 128 devices: a whole 4x4x4 slice. The times are simulated.
128 devices in a mesh: dp: 8 (over y_hi, z), seq: 16 (over x, y_lo, core).
Axes of the slice: x: 4, y: 4 (y_hi: 2, y_lo: 2; y = y_hi * 2 + y_lo), z: 4, core: 2. Of those that a mesh axis runs over, the one named last changes fastest.
Arguments:
- points: bfloat16 [8, 16384, 512], P('dp', 'seq'), may hold values from -6 to 6
- ball_lists: int32 [8, 16384], P('dp', 'seq'), may hold values from 0 to 1023, as said below
- gains: float32 [2, 512], replicated, may hold values from 0.25 to 1.75
- w_qkv: bfloat16 [2, 512, 1536], replicated, may hold values from -0.25 to 0.25
- w_out: bfloat16 [2, 512, 512], replicated, may hold values from -0.25 to 0.25
- cotangent: bfloat16 [8, 16384, 512], P('dp', 'seq'), may hold values from -6 to 6
Outputs:
- mixed: bfloat16 [8, 16384, 512], P('dp', 'seq')
- grad_points: bfloat16 [8, 16384, 512], P('dp', 'seq')
- grad_gains: float32 [2, 512], replicated
- grad_qkv: float32 [2, 512, 1536], replicated
- grad_out: float32 [2, 512, 512], replicated
Inputs may be any that keep to these rules, and one draw needn't show every extreme that they name: `ball_lists`: for each snapshot and each index s of seq, its 1024 entries are a permutation of 0 to 1023; so every rotated block of 1024 positions takes exactly 64 points from each index of seq.
All inputs are finite; a program needn't handle non-finite values.
Results may differ from a plain program's by a relative error of at most 0.017.
Values may be sent and summed in bfloat16 or wider, within the bound.
A program may use at most 128 MiB of HBM per device.

v0:
```python
import jax
import jax.numpy as jnp
from jax import lax
from jax.experimental import pallas as pl
from jax.experimental.pallas import tpu as pltpu
from jax.sharding import PartitionSpec as P

HEADS = 8
BALL = 256
EPS = 1e-05
F32 = jnp.float32
BF16 = jnp.bfloat16
VMEM_BYTES = 60 * 1024 * 1024


def dot(a, b, ca, cb):
    return lax.dot_general(a, b, (((ca,), (cb,)), ((), ())), preferred_element_type=F32)


def nn(a, b):
    return dot(a, b, 1, 0)


def nt(a, b):
    return dot(a, b, 1, 1)


def tn(a, b):
    return dot(a, b, 0, 0)


def cols(ball):
    return pl.ds(pl.multiple_of(ball * BALL, BALL), BALL)


def norm_scale(x):
    return lax.rsqrt(jnp.mean(x * x, axis=1, keepdims=True) + EPS)


def one_hot_to_rotated(order_row, first):
    rows = order_row.shape[1]
    lane = 128
    held = jnp.broadcast_to(order_row[:, pl.ds(pl.multiple_of(first, lane), lane)], (lane, lane)).T
    row = lax.broadcasted_iota(jnp.int32, (lane, lane), 1)
    parts = [jnp.where(held == row + low, 1.0, 0.0).astype(BF16) for low in range(0, rows, lane)]
    return jnp.concatenate(parts, axis=1)


def one_hot_to_tree(order_row, first, rows):
    tree = lax.broadcasted_iota(jnp.int32, (rows, order_row.shape[1]), 0) + first
    return jnp.where(order_row[...] == tree, 1.0, 0.0).astype(BF16)


def transpose_by_unit(wqkv, wqkv_t):
    unit = jnp.where(
        lax.broadcasted_iota(jnp.int32, (BALL, BALL), 0) == lax.broadcasted_iota(jnp.int32, (BALL, BALL), 1), 1.0, 0.0
    ).astype(BF16)
    for low in range(0, wqkv.shape[1], BALL):
        wqkv_t[low : low + BALL, :] = nt(unit, wqkv[:, low : low + BALL]).astype(BF16)


def forward_ball(ball, x, gain, wqkv_t, wout, h_t, qkv_t, p_t, att_t, inv):
    width = x.shape[1]
    size = width // HEADS
    here = cols(ball)
    values = x.astype(F32)
    hidden = (values * norm_scale(values) * gain).astype(BF16)
    hidden_t = hidden.T
    h_t[:, here] = hidden_t
    qkv_t[:, here] = nn(wqkv_t[...], hidden_t).astype(BF16)
    for head in range(HEADS):
        low = head * size
        q = qkv_t[low : low + size, here] * size ** (-0.5)
        k = qkv_t[width + low : width + low + size, here]
        v = qkv_t[2 * width + low : 2 * width + low + size, here]
        scores = tn(k, q)
        weights = jnp.exp(scores - jnp.max(scores, axis=0, keepdims=True))
        share = 1.0 / jnp.sum(weights, axis=0, keepdims=True)
        weights = weights.astype(BF16)
        p_t[ball, head] = weights
        inv[ball, head : head + 1, :] = share
        att_t[low : low + size, here] = (nn(v, weights) * share).astype(BF16)
    return values + tn(att_t[:, here], wout[...])


def backward_ball(ball, x, gain, dy, wqkv, wout, qkv_t, p_t, att_t, inv, dqkv_t):
    width = x.shape[1]
    size = width // HEADS
    here = cols(ball)
    d_att = nt(wout[...], dy).astype(BF16)
    for head in range(HEADS):
        low = head * size
        q = qkv_t[low : low + size, here] * size ** (-0.5)
        k = qkv_t[width + low : width + low + size, here]
        v = qkv_t[2 * width + low : 2 * width + low + size, here]
        share = inv[ball, head : head + 1, :]
        d_out = d_att[low : low + size].astype(F32) * share
        delta = jnp.sum(d_out * att_t[low : low + size, here].astype(F32), axis=0, keepdims=True)
        d_out = d_out.astype(BF16)
        weights = p_t[ball, head]
        d_scores = (weights.astype(F32) * (tn(v, d_out) - delta)).astype(BF16)
        dqkv_t[low : low + size, here] = (nn(k, d_scores) * size ** (-0.5)).astype(BF16)
        dqkv_t[width + low : width + low + size, here] = nt(q, d_scores).astype(BF16)
        dqkv_t[2 * width + low : 2 * width + low + size, here] = nt(d_out, weights).astype(BF16)
    d_h = nn(wqkv[...], dqkv_t[:, here]).T
    values = x.astype(F32)
    scale = norm_scale(values)
    unit = values * scale
    d_unit = d_h * gain
    d_n = scale * (d_unit - unit * jnp.mean(d_unit * unit, axis=1, keepdims=True))
    d_x = dy.astype(F32) + d_n.astype(BF16).astype(F32)
    return d_x.astype(BF16), jnp.sum(d_h * unit, axis=0, keepdims=True)


TO_X, TO_COT, BACK_R, BACK_D = range(4)
MESH = pl.DeviceIdType.MESH


def kernel(
    points, lists, gains, w_qkv, w_out, cotangent,
    mixed_out, points_out, gain_out, qkv_out, out_out,
    order, x, cot, gain, wqkv, wout, wqkv_t, place, y,
    h0, qkv0, p0, att0, inv0, h1, qkv1, p1, att1, inv1, dqkv, d_y,
    sent, got, mixed, d_x, g_gain, g_qkv, g_out,
    load_sem, store_sem, send_sem, recv_sem,
):
    groups = lax.axis_size("seq")
    me = lax.axis_index("seq")
    rows = x.shape[0]
    block = rows // groups
    balls = rows // BALL
    near = groups // balls
    home = me // near
    seat = me % near

    loads = []

    def load(source, target):
        copy = pltpu.make_async_copy(source, target, load_sem.at[len(loads)])
        copy.start()
        loads.append(copy)
        return copy

    lists_in = load(lists, order)
    cot_in = load(cotangent.at[0], cot)
    x_in = load(points.at[0], x)
    small_in = [load(gains, gain), load(w_qkv.at[0], wqkv.at[0]), load(w_out.at[0], wout.at[0])]
    late_in = [load(w_qkv.at[1], wqkv.at[1]), load(w_out.at[1], wout.at[1])]

    barrier = pltpu.get_barrier_semaphore()
    for step in range(1, groups):
        pl.semaphore_signal(barrier, inc=1, device_id={"seq": (me + step) % groups}, device_id_type=MESH)

    def span(index):
        return pl.ds(pl.multiple_of(index * block, block), block)

    def transfer(kind, source, peer):
        return pltpu.make_async_remote_copy(
            src_ref=sent.at[kind, span(peer), :],
            dst_ref=got.at[kind, span(source), :],
            send_sem=send_sem.at[kind, peer],
            recv_sem=recv_sem.at[kind, source],
            device_id={"seq": peer},
            device_id_type=MESH,
        )

    def send_home(kind):
        got[kind, span(me), :] = sent[kind, span(me), :]
        for step in range(1, near):
            transfer(kind, me, home * near + (seat + step) % near).start()

    def send_away(kind, group):
        for step in range(near):
            transfer(kind, me, group * near + (seat + step) % near).start()

    def arrive_home(kind):
        for step in range(1, near):
            transfer(kind, home * near + (seat + step) % near, me).wait_recv()

    def arrive_away(kind, group):
        for step in range(near):
            transfer(kind, group * near + step, me).wait_recv()

    def gather(kind, source, group):
        sent[kind, cols(group), :] = nn(place[cols(group), :], source[...]).astype(BF16)

    lists_in.wait()

    @pl.loop(0, rows // 128)
    def _(part):
        first = pl.multiple_of(part * 128, 128)
        place[pl.ds(first, 128), :] = one_hot_to_rotated(order, first)

    cot_in.wait()
    pl.semaphore_wait(barrier, groups - 1)
    gather(TO_COT, cot, home)
    send_home(TO_COT)

    @pl.loop(1, balls)
    def _(step):
        group = (home + step) % balls
        gather(TO_COT, cot, group)
        send_away(TO_COT, group)

    x_in.wait()
    for copy in small_in:
        copy.wait()
    transpose_by_unit(wqkv.at[0], wqkv_t.at[0])

    @pl.loop(0, balls)
    def _(ball):
        y[cols(ball), :] = forward_ball(
            ball, x[cols(ball), :], gain[0:1], wqkv_t.at[0], wout.at[0], h0, qkv0, p0, att0, inv0
        ).astype(BF16)

    gather(TO_X, y, home)
    send_home(TO_X)

    @pl.loop(1, balls)
    def _(step):
        group = (home + step) % balls
        gather(TO_X, y, group)
        send_away(TO_X, group)

    for copy in late_in:
        copy.wait()
    transpose_by_unit(wqkv.at[1], wqkv_t.at[1])
    g_gain[...] = jnp.zeros_like(g_gain)

    def forward_rotated(ball):
        sent[BACK_R, cols(ball), :] = forward_ball(
            ball, got[TO_X, cols(ball), :], gain[1:2], wqkv_t.at[1], wout.at[1], h1, qkv1, p1, att1, inv1
        ).astype(BF16)

    def backward_rotated(ball):
        sent[BACK_D, cols(ball), :], gained = backward_ball(
            ball, got[TO_X, cols(ball), :], gain[1:2], got[TO_COT, cols(ball), :],
            wqkv.at[1], wout.at[1], qkv1, p1, att1, inv1, dqkv,
        )
        g_gain[1:2] += gained

    arrive_home(TO_X)
    forward_rotated(home)
    send_home(BACK_R)

    @pl.loop(1, balls)
    def _(step):
        ball = (home + step) % balls
        arrive_away(TO_X, ball)
        forward_rotated(ball)
        send_away(BACK_R, ball)
        arrive_away(TO_COT, ball)
        backward_rotated(ball)
        send_away(BACK_D, ball)

    arrive_home(TO_COT)
    backward_rotated(home)
    send_home(BACK_D)

    stores = []

    def store(source, target):
        copy = pltpu.make_async_copy(source, target, store_sem.at[len(stores)])
        copy.start()
        stores.append(copy)
        return copy

    g_out[...] = nn(att1[...], got[TO_COT])
    out_copy = store(g_out, out_out.at[1])
    g_qkv[...] = nt(h1[...], dqkv[...])
    qkv_copy = store(g_qkv, qkv_out.at[1])

    def arrive(kind):
        arrive_home(kind)

        @pl.loop(1, balls)
        def _(step):
            arrive_away(kind, (home + step) % balls)

    arrive(BACK_R)

    @pl.loop(0, balls)
    def _(ball):
        mixed[cols(ball), :] = nn(one_hot_to_tree(order, ball * BALL, BALL), got[BACK_R]).astype(BF16)

    mixed_copy = store(mixed, mixed_out.at[0])
    arrive(BACK_D)

    @pl.loop(0, balls)
    def _(ball):
        d_y[cols(ball), :] = nn(one_hot_to_tree(order, ball * BALL, BALL), got[BACK_D]).astype(BF16)
        d_x[cols(ball), :], gained = backward_ball(
            ball, x[cols(ball), :], gain[0:1], d_y[cols(ball), :],
            wqkv.at[0], wout.at[0], qkv0, p0, att0, inv0, dqkv,
        )
        g_gain[0:1] += gained

    store(d_x, points_out.at[0])
    store(g_gain, gain_out)
    out_copy.wait()
    g_out[...] = nn(att0[...], d_y[...])
    store(g_out, out_out.at[0])
    qkv_copy.wait()
    g_qkv[...] = nt(h0[...], dqkv[...])
    store(g_qkv, qkv_out.at[0])
    for copy in stores:
        if copy is not out_copy and copy is not qkv_copy:
            copy.wait()

    @pl.loop(1, groups)
    def _(step):
        peer = (me + step) % groups
        for kind in range(4):
            transfer(kind, me, peer).wait_send()


def local(points, ball_lists, gains, w_qkv, w_out, cotangent):
    groups = lax.axis_size("seq")
    rows, width = points.shape[1:]
    balls = rows // BALL
    any_place = pl.BlockSpec(memory_space=pl.ANY)
    saved = [
        pltpu.VMEM((width, rows), BF16),
        pltpu.VMEM((3 * width, rows), BF16),
        pltpu.VMEM((balls, HEADS, BALL, BALL), BF16),
        pltpu.VMEM((width, rows), BF16),
        pltpu.VMEM((balls, HEADS, BALL), F32),
    ]
    token = pltpu.VMEM((rows, width), BF16)
    mixed, d_x, *grads = pl.pallas_call(
        kernel,
        out_shape=[
            jax.ShapeDtypeStruct(points.shape, BF16),
            jax.ShapeDtypeStruct(points.shape, BF16),
            jax.ShapeDtypeStruct(gains.shape, F32),
            jax.ShapeDtypeStruct(w_qkv.shape, F32),
            jax.ShapeDtypeStruct(w_out.shape, F32),
        ],
        in_specs=[any_place] * 6,
        out_specs=[any_place] * 5,
        scratch_shapes=[
            pltpu.VMEM((1, rows), jnp.int32),
            token,
            token,
            pltpu.VMEM(gains.shape, F32),
            pltpu.VMEM(w_qkv.shape, BF16),
            pltpu.VMEM(w_out.shape, BF16),
            pltpu.VMEM((2, 3 * width, width), BF16),
            pltpu.VMEM((rows, rows), BF16),
            token,
            *saved,
            *saved,
            pltpu.VMEM((3 * width, rows), BF16),
            token,
            pltpu.VMEM((4, rows, width), BF16),
            pltpu.VMEM((4, rows, width), BF16),
            token,
            token,
            pltpu.VMEM(gains.shape, F32),
            pltpu.VMEM((width, 3 * width), F32),
            pltpu.VMEM((width, width), F32),
            pltpu.SemaphoreType.DMA((8,)),
            pltpu.SemaphoreType.DMA((8,)),
            pltpu.SemaphoreType.DMA((4, groups)),
            pltpu.SemaphoreType.DMA((4, groups)),
        ],
        compiler_params=pltpu.CompilerParams(
            vmem_limit_bytes=VMEM_BYTES, collective_id=0, has_side_effects=True
        ),
    )(points, ball_lists, gains, w_qkv, w_out, cotangent)
    totals = lax.psum(tuple(grads), ("dp", "seq"))
    return (mixed, d_x, *totals)


def solution(mesh):
    return jax.shard_map(
        local,
        mesh=mesh,
        in_specs=(P("dp", "seq", None), P("dp", "seq"), P(), P(), P(), P("dp", "seq", None)),
        out_specs=(P("dp", "seq", None), P("dp", "seq", None), P(), P(), P()),
        check_vma=False,
    )
```

profile of v0, /device:TPU:1, one launch (start us, length us, event | category | flops | bytes accessed | tf_op | source)
XLA Modules:
  0.0 279.4 jit_solution(11727267690258114995)
XLA Ops:
  7.2 0.0 all-reduce.3.cloned.1.call-start
  7.2 92.5 %shard_map.101 = (bf16[1,1024,512]{2,1,0:T(8,128)(2,1)}, bf16[1,1024,512]{2,1,0:T(8,128)(2,1)}, f32[2,512]{1,0:T(2,128)}, f32[2,512,1536]{2,1,0:T(8,128)}, f32[2,512,512]{2,1,0:T(8,128)}) custom-call(bf16[1,1024,512]{2,1,0:T(8,128)(2,1)} %points.1, s32[1,1024]{1,0:T(1,128)} %lists.1, f32[2,512]{1,0:T(2,128)} %gains.1, bf16[2,512,1536]{2,1,0:T(8,128)(2,1)} %w_qkv.1, ...), custom_call_target="tpu_custom_call" | custom-call | tf_op jit(solution)/shard_map/pallas_call | solution.py:330
  99.8 0.0 copy-start.3
  99.8 0.0 copy-start.2
  99.8 0.0 copy-start.1
  99.8 0.0 all-reduce.3.cloned.1.call-update
  99.8 0.6 copy-done.3
  100.4 66.3 %psum.21 = f32[2,512]{1,0:T(2,128)} all-reduce(f32[2,512]{1,0:T(2,128)S(1)} %copy-done.3), channel_id=1, replica_groups=mesh['dp'=8,'seq'=16] {'dp','seq'}, use_global_device_ids=true, to_apply=%region_0.0 | all-reduce | flops 1024 | bytes 8192 | tf_op jit(solution)/shard_map/psum | solution.py:371
  166.7 96.5 %all-reduce.3.cloned.1.call-done = (f32[2,512,1536]{2,1,0:T(8,128)}, f32[2,512,512]{2,1,0:T(8,128)}) async-done(((f32[2,512,1536]{2,1,0:T(8,128)}, f32[2,512,512]{2,1,0:T(8,128)}), (f32[2,512,1536]{2,1,0:T(8,128)}, f32[2,512,512]{2,1,0:T(8,128)})) %all-reduce.3.cloned.1.call-update) | async-done | bytes 8388624 | tf_op jit(solution)/shard_map/psum | solution.py:371
  263.3 0.0 copy-done.2
  263.3 1.0 copy.17
  264.2 0.0 copy-done.1
  264.2 1.0 copy.18
  265.2 0.0 copy-start
  265.2 6.1 %copy.19 = f32[2,512,1536]{2,1,0:T(8,128)} copy(f32[2,512,1536]{2,1,0:T(8,128)} %get-tuple-element.25) | data formatting | bytes 12582912
  271.3 0.0 copy-done
  271.3 1.3 copy.20
Async XLA Ops:
  7.2 256.1 %all-reduce.3.cloned.1.call-start = ((), (), s32[]{:S(2)}) async-start(), calls=%async_computation | async-start | bytes 16777216 | tf_op jit(solution)/shard_map/psum | solution.py:371
  99.8 0.7 copy-start.3
  99.8 163.5 %copy-start.2 = (bf16[1,1024,512]{2,1,0:T(8,128)(2,1)S(1)}, bf16[1,1024,512]{2,1,0:T(8,128)(2,1)}, u32[]{:S(2)}) copy-start(bf16[1,1024,512]{2,1,0:T(8,128)(2,1)} %get-tuple-element.22) | copy-start | bytes 3145732
  99.8 164.5 %copy-start.1 = (bf16[1,1024,512]{2,1,0:T(8,128)(2,1)S(1)}, bf16[1,1024,512]{2,1,0:T(8,128)(2,1)}, u32[]{:S(2)}) copy-start(bf16[1,1024,512]{2,1,0:T(8,128)(2,1)} %get-tuple-element.23) | copy-start | bytes 3145732
  265.2 6.1 %copy-start = (f32[2,512,512]{2,1,0:T(8,128)S(1)}, f32[2,512,512]{2,1,0:T(8,128)}, u32[]{:S(2)}) copy-start(f32[2,512,512]{2,1,0:T(8,128)} %get-tuple-element.26) | copy-start | bytes 6291460
Sparse Core Ops, SparseCore 0:
  99.9 163.2 all-reduce.2
where the time goes:
time: 280 us; the launch traced here: 279 us
  waiting for transfers between devices  96.5 us (34%)
  Pallas kernels  92.5 us (33%)
  blocking collectives  66.3 us (24%)
  between operations  14.1 us (5%)
  local copies, waits for them, and re-layouts  9.98 us (4%)
    psum x1, waiting for transfers between devices, local(): totals = lax.psum(tuple(grads), ('dp', 'seq'))  96.5 us
    pallas_call x1, Pallas kernels, local(): pl.pallas_call(kernel, out_shape=[jax.ShapeDtypeStruct(points.shape, BF16...  92.5 us
    psum x1, blocking collectives, local(): totals = lax.psum(tuple(grads), ('dp', 'seq'))  66.3 us
    unnamed x12, local copies, waits for them, and re-layouts  9.98 us
  transfers between devices with their start and end apart: 1, of which 1 were waited for; matrix products, arithmetic and copies ran while one was open for 0% of the time, Pallas kernels for 0%

commit v1 on v0

v1 whole, which is shorter than its diff:
```python
import jax
import jax.numpy as jnp
from jax import lax
from jax.experimental import pallas as pl
from jax.experimental.pallas import tpu as pltpu
from jax.sharding import PartitionSpec as P

MESH = pl.DeviceIdType.MESH
HEADS = 8
BALL = 256
EPS = 1e-05
F32 = jnp.float32
BF16 = jnp.bfloat16
VMEM_BYTES = 62 * 1024 * 1024


def dot(a, b, ca, cb):
    return lax.dot_general(a, b, (((ca,), (cb,)), ((), ())), preferred_element_type=F32)


def nn(a, b):
    return dot(a, b, 1, 0)


def nt(a, b):
    return dot(a, b, 1, 1)


def tn(a, b):
    return dot(a, b, 0, 0)


def cols(ball):
    return pl.ds(pl.multiple_of(ball * BALL, BALL), BALL)


def norm_scale(x):
    return lax.rsqrt(jnp.mean(x * x, axis=1, keepdims=True) + EPS)


def one_hot_to_rotated(order_row, first):
    rows = order_row.shape[1]
    lane = 128
    held = jnp.broadcast_to(order_row[:, pl.ds(pl.multiple_of(first, lane), lane)], (lane, lane)).T
    row = lax.broadcasted_iota(jnp.int32, (lane, lane), 1)
    parts = [jnp.where(held == row + low, 1.0, 0.0).astype(BF16) for low in range(0, rows, lane)]
    return jnp.concatenate(parts, axis=1)


def one_hot_to_tree(order_row, first, rows):
    tree = lax.broadcasted_iota(jnp.int32, (rows, order_row.shape[1]), 0) + first
    return jnp.where(order_row[...] == tree, 1.0, 0.0).astype(BF16)


def transpose_by_unit(wqkv, wqkv_t):
    unit = jnp.where(
        lax.broadcasted_iota(jnp.int32, (BALL, BALL), 0) == lax.broadcasted_iota(jnp.int32, (BALL, BALL), 1), 1.0, 0.0
    ).astype(BF16)
    for low in range(0, wqkv.shape[1], BALL):
        wqkv_t[low : low + BALL, :] = nt(unit, wqkv[:, low : low + BALL]).astype(BF16)


def forward_ball(ball, keep, x, gain, wqkv_t, wout, h_t, qkv_t, p_t, att_t, inv):
    width = x.shape[1]
    size = width // HEADS
    here = cols(ball)
    values = x.astype(F32)
    hidden = (values * norm_scale(values) * gain).astype(BF16)
    hidden_t = hidden.T
    h_t[:, here] = hidden_t
    qkv_t[:, here] = nn(wqkv_t[...], hidden_t).astype(BF16)
    for head in range(HEADS):
        low = head * size
        q = qkv_t[low : low + size, here] * size ** (-0.5)
        k = qkv_t[width + low : width + low + size, here]
        v = qkv_t[2 * width + low : 2 * width + low + size, here]
        scores = tn(k, q)
        weights = jnp.exp(scores - jnp.max(scores, axis=0, keepdims=True))
        share = 1.0 / jnp.sum(weights, axis=0, keepdims=True)
        weights = weights.astype(BF16)
        p_t[keep, head] = weights
        inv[keep, head : head + 1, :] = share
        att_t[low : low + size, here] = (nn(v, weights) * share).astype(BF16)
    return values + tn(att_t[:, here], wout[...])


def backward_heads(ball, keep, heads, d_att, qkv_t, p_t, att_t, inv, dqkv_t):
    width = d_att.shape[0]
    size = width // HEADS
    here = cols(ball)
    for head in heads:
        low = head * size
        q = qkv_t[low : low + size, here] * size ** (-0.5)
        k = qkv_t[width + low : width + low + size, here]
        v = qkv_t[2 * width + low : 2 * width + low + size, here]
        share = inv[keep, head : head + 1, :]
        d_out = d_att[low : low + size, here].astype(F32) * share
        delta = jnp.sum(d_out * att_t[low : low + size, here].astype(F32), axis=0, keepdims=True)
        d_out = d_out.astype(BF16)
        weights = p_t[keep, head]
        d_scores = (weights.astype(F32) * (tn(v, d_out) - delta)).astype(BF16)
        dqkv_t[low : low + size, here] = (nn(k, d_scores) * size ** (-0.5)).astype(BF16)
        dqkv_t[width + low : width + low + size, here] = nt(q, d_scores).astype(BF16)
        dqkv_t[2 * width + low : 2 * width + low + size, here] = nt(d_out, weights).astype(BF16)


def backward_norm(ball, x, gain, dy, wqkv, dqkv_t):
    d_h = nn(wqkv[...], dqkv_t[:, cols(ball)]).T
    values = x.astype(F32)
    scale = norm_scale(values)
    unit = values * scale
    d_unit = d_h * gain
    d_n = scale * (d_unit - unit * jnp.mean(d_unit * unit, axis=1, keepdims=True))
    d_x = dy.astype(F32) + d_n.astype(BF16).astype(F32)
    return d_x.astype(BF16), jnp.sum(d_h * unit, axis=0, keepdims=True)


class Place:
    def __init__(self):
        dp, seq = lax.axis_index("dp"), lax.axis_index("seq")
        self.at = {"x": seq // 4, "y": dp // 4 * 2 + seq // 2 % 2, "z": dp % 4, "core": seq % 2}
        sizes = {"x": 4, "y": 4, "z": 4, "core": 2}
        self.peers = {
            axis: [(self.at[axis] + step) % size for step in range(1, size)] for axis, size in sizes.items()
        }

    def other(self, axis, value):
        at = {**self.at, axis: value}
        return {"dp": at["y"] // 2 * 4 + at["z"], "seq": at["x"] * 4 + at["y"] % 2 * 2 + at["core"]}


SCATTER = (0, 2, 6)
LAST = 10
GATHER = (22, 18, 14)
SUM_SEMS = 24


class Sum:
    def __init__(self, place, slot, axes, part, total, halves, quarters, pieces, lasts, send_sem, recv_sem):
        self.place, self.slot, self.axes = place, slot, axes
        self.part, self.total = part, total
        self.inboxes, self.lasts = [halves, quarters, pieces], lasts
        self.send_sem, self.recv_sem = send_sem, recv_sem
        rows = part.shape[0]
        self.sizes = [rows, rows // 2, rows // 8, rows // 32]
        self.names = ["core", axes[0], axes[1]]
        base, self.bases = 0, [0]
        for size, name in zip(self.sizes[1:], self.names):
            base = base + place.at[name] * size
            self.bases.append(base)
        self.done = 0

    def span(self, level, coordinate=None):
        base = self.bases[level] if coordinate is None else self.bases[level - 1] + coordinate * self.sizes[level]
        return pl.ds(pl.multiple_of(base, 16), self.sizes[level])

    def hop(self, first, axis, source, target, here, there):
        return pltpu.make_async_remote_copy(
            src_ref=source,
            dst_ref=target,
            send_sem=self.send_sem.at[self.slot, first + there],
            recv_sem=self.recv_sem.at[self.slot, first + here],
            device_id=self.place.other(axis, there),
            device_id_type=MESH,
        )

    def scatter(self, level, here, there):
        axis = self.names[level - 1]
        inbox = self.inboxes[level - 1].at[0 if level == 1 else here]
        return self.hop(SCATTER[level - 1], axis, self.part.at[self.span(level, there), :], inbox, here, there)

    def exchange(self, here, there):
        return self.hop(LAST, self.axes[2], self.lasts.at[here], self.lasts.at[here], here, there)

    def gather(self, level, here, there):
        rows = self.total.at[self.span(level, here), :]
        return self.hop(GATHER[level - 1], self.names[level - 1], rows, rows, here, there)

    def start(self, kind, axis, *level):
        for peer in self.place.peers[axis]:
            kind(*level, self.place.at[axis], peer).start()

    def arrive(self, kind, axis, *level):
        for peer in self.place.peers[axis]:
            kind(*level, peer, self.place.at[axis]).wait_recv()

    def left(self, kind, axis, *level):
        for peer in self.place.peers[axis]:
            kind(*level, self.place.at[axis], peer).wait_send()

    def added(self, level):
        axis = self.names[level - 1]
        self.arrive(self.scatter, axis, level)
        value = self.part[self.span(level), :].astype(F32)
        for peer in self.place.peers[axis]:
            value += self.inboxes[level - 1][0 if level == 1 else peer].astype(F32)
        return value.astype(BF16)

    def step(self):
        step, self.done = self.done, self.done + 1
        last = self.axes[2]
        if step == 0:
            self.start(self.scatter, self.names[0], 1)
        elif step in (1, 2):
            self.part[self.span(step), :] = self.added(step)
            self.start(self.scatter, self.names[step], step + 1)
        elif step == 3:
            self.lasts[self.place.at[last]] = self.added(3)
            self.start(self.exchange, last)
        elif step == 4:
            self.arrive(self.exchange, last)
            value = self.lasts[0].astype(F32)
            for peer in range(1, 4):
                value += self.lasts[peer].astype(F32)
            self.total[self.span(3), :] = value.astype(BF16)
            self.start(self.gather, self.names[2], 3)
        elif step in (5, 6):
            self.arrive(self.gather, self.names[7 - step], 8 - step)
            self.start(self.gather, self.names[6 - step], 7 - step)
        elif step == 7:
            self.arrive(self.gather, self.names[0], 1)

    def clear(self):
        for level in (1, 2, 3):
            self.left(self.scatter, self.names[level - 1], level)
            self.left(self.gather, self.names[level - 1], level)
        self.left(self.exchange, self.axes[2])


class SmallSum:
    axes = ("core", "x", "y", "z")

    def __init__(self, place, boxes, send_sem, recv_sem):
        self.place, self.boxes, self.send_sem, self.recv_sem = place, boxes, send_sem, recv_sem
        self.done = 0

    def hop(self, step, here, there):
        box = self.boxes.at[step, here]
        return pltpu.make_async_remote_copy(
            src_ref=box,
            dst_ref=box,
            send_sem=self.send_sem.at[step, there],
            recv_sem=self.recv_sem.at[step, here],
            device_id=self.place.other(self.axes[step], there),
            device_id_type=MESH,
        )

    def send(self, value):
        axis = self.axes[self.done]
        mine = self.place.at[axis]
        self.boxes[self.done, mine] = value
        for peer in self.place.peers[axis]:
            self.hop(self.done, mine, peer).start()

    def receive(self):
        axis = self.axes[self.done]
        for peer in self.place.peers[axis]:
            self.hop(self.done, peer, self.place.at[axis]).wait_recv()
        value = self.boxes[self.done, 0]
        for peer in range(1, len(self.place.peers[axis]) + 1):
            value += self.boxes[self.done, peer]
        self.done += 1
        return value

    def clear(self):
        for step, axis in enumerate(self.axes):
            for peer in self.place.peers[axis]:
                self.hop(step, self.place.at[axis], peer).wait_send()


TO_X, TO_COT, BACK_R, BACK_D = range(4)
GROUPS = 2
SUMS = (
    (1024, ("x", "z", "y")),
    (1024, ("z", "x", "y")),
    (512, ("z", "x", "y")),
    (768, ("x", "z", "y")),
    (256, ("x", "z", "y")),
    (256, ("z", "y", "x")),
    (256, ("y", "x", "z")),
)


def kernel(
    points, lists, gains, w_qkv, w_out, cotangent,
    mixed_out, points_out, gain_out, qkv_out, out_out,
    order, x, cot, gain, wqkv, wout, wqkv_t, onto, y,
    h0, qkv0, p0, att0, inv0, h1, qkv1, p1, att1, inv1, dqkv, d_att,
    sent, got, d_x, g_gain, *rest,
):
    sum_boxes, rest = rest[: 6 * len(SUMS)], rest[6 * len(SUMS) :]
    boxes, load_sem, store_sem, send_sem, recv_sem, sum_send, sum_recv, small_send, small_recv = rest
    groups = lax.axis_size("seq")
    me = lax.axis_index("seq")
    rows = x.shape[0]
    block = rows // groups
    balls = rows // BALL
    near = groups // balls
    home = me // near
    seat = me % near
    place = Place()
    sums = [
        Sum(place, slot, axes, *sum_boxes[6 * slot : 6 * slot + 6], sum_send, sum_recv)
        for slot, (columns, axes) in enumerate(SUMS)
    ]
    upper, sum_o, sum_q, last = sums[0:2], sums[2], sums[3], sums[4:7]
    small = SmallSum(place, boxes, small_send, small_recv)

    loads = []

    def load(source, target):
        copy = pltpu.make_async_copy(source, target, load_sem.at[len(loads)])
        copy.start()
        loads.append(copy)
        return copy

    lists_in = load(lists, order)
    cot_in = load(cotangent.at[0], cot)
    x_in = load(points.at[0], x)
    small_in = [load(gains, gain), load(w_qkv.at[0], wqkv.at[0]), load(w_out.at[0], wout.at[0])]
    late_in = [load(w_qkv.at[1], wqkv.at[1]), load(w_out.at[1], wout.at[1])]

    barrier = pltpu.get_barrier_semaphore()
    for step in range(1, near):
        pl.semaphore_signal(
            barrier, inc=1, device_id={"seq": home * near + (seat + step) % near}, device_id_type=MESH
        )
    for axis in ("x", "z"):
        for peer in place.peers[axis]:
            pl.semaphore_signal(barrier, inc=1, device_id=place.other(axis, peer), device_id_type=MESH)
    for step in range(2):
        far = (place.at["y"] // 2 * 2 + 2 + step) % 4
        pl.semaphore_signal(barrier, inc=1, device_id=place.other("y", far), device_id_type=MESH)

    def span(index):
        return pl.ds(pl.multiple_of(index * block, block), block)

    others = [(seat + step) % near for step in range(1, near)]

    def transfer(kind, ball, here, there):
        return pltpu.make_async_remote_copy(
            src_ref=sent.at[kind, span(ball * near + there), :],
            dst_ref=got.at[kind, span(ball * near + here), :],
            send_sem=send_sem.at[kind, ball * near + there],
            recv_sem=recv_sem.at[kind, ball * near + here],
            device_id={"seq": home * near + there},
            device_id_type=MESH,
        )

    def send(kind, ball):
        for peer in others:
            transfer(kind, ball, seat, peer).start()
        own = span(ball * near + seat)
        got[kind, own, :] = sent[kind, own, :]

    def arrive(kind, ball):
        for peer in others:
            transfer(kind, ball, peer, seat).wait_recv()

    def gather(kind, source, group):
        sent[kind, cols(group), :] = nn(onto[cols(group), :], source[...]).astype(BF16)

    lists_in.wait()

    @pl.loop(0, rows // 128)
    def _(part):
        first = pl.multiple_of(part * 128, 128)
        onto[pl.ds(first, 128), :] = one_hot_to_rotated(order, first)

    cot_in.wait()
    pl.semaphore_wait(barrier, near - 1 + 8)

    @pl.loop(0, balls)
    def _(ball):
        gather(TO_COT, cot, ball)
        send(TO_COT, ball)

    x_in.wait()
    for copy in small_in:
        copy.wait()
    transpose_by_unit(wqkv.at[0], wqkv_t.at[0])

    @pl.loop(0, balls)
    def _(ball):
        y[cols(ball), :] = forward_ball(
            ball, ball, x[cols(ball), :], gain[0:1], wqkv_t.at[0], wout.at[0], h0, qkv0, p0, att0, inv0
        ).astype(BF16)

    @pl.loop(0, balls)
    def _(ball):
        gather(TO_X, y, ball)
        send(TO_X, ball)

    for copy in late_in:
        copy.wait()
    transpose_by_unit(wqkv.at[1], wqkv_t.at[1])
    g_gain[...] = jnp.zeros_like(g_gain)

    @pl.loop(0, balls)
    def _(ball):
        arrive(TO_X, ball)
        rows_x = got[TO_X, cols(ball), :]
        sent[BACK_R, cols(ball), :] = forward_ball(
            ball, 0, rows_x, gain[1:2], wqkv_t.at[1], wout.at[1], h1, qkv1, p1, att1, inv1
        ).astype(BF16)
        send(BACK_R, ball)
        arrive(TO_COT, ball)
        d_r = got[TO_COT, cols(ball), :]
        d_att[:, cols(ball)] = nt(wout[1], d_r).astype(BF16)
        backward_heads(ball, 0, range(HEADS), d_att, qkv1, p1, att1, inv1, dqkv)
        sent[BACK_D, cols(ball), :], gained = backward_norm(
            ball, got[TO_X, cols(ball), :], gain[1:2], d_r, wqkv.at[1], dqkv
        )
        send(BACK_D, ball)
        g_gain[1:2] += gained

    stores = []

    def store(source, target):
        copy = pltpu.make_async_copy(source, target, store_sem.at[len(stores)])
        copy.start()
        stores.append(copy)
        return copy

    width = x.shape[1]
    first, second = upper[0].part, upper[1].part
    second[:, width:] = nn(att1[...], got[TO_COT]).astype(BF16)
    first[...] = nt(h1[...], dqkv[: 2 * width, :]).astype(BF16)
    second[:, :width] = nt(h1[...], dqkv[2 * width :, :]).astype(BF16)

    def advance(*which):
        for each in which:
            each.step()

    advance(*upper)

    @pl.loop(0, balls)
    def _(ball):
        arrive(BACK_R, ball)

    @pl.loop(0, balls)
    def _(ball):
        cot[cols(ball), :] = nn(one_hot_to_tree(order, ball * BALL, BALL), got[BACK_R]).astype(BF16)

    store(cot, mixed_out.at[0])
    advance(*upper)

    @pl.loop(0, balls)
    def _(ball):
        arrive(BACK_D, ball)

    @pl.loop(0, balls)
    def _(ball):
        y[cols(ball), :] = nn(one_hot_to_tree(order, ball * BALL, BALL), got[BACK_D]).astype(BF16)
        d_att[:, cols(ball)] = nt(wout[0], y[cols(ball), :]).astype(BF16)

    sum_o.part[...] = nn(att0[...], y[...]).astype(BF16)
    advance(sum_o)
    span_q = width // GROUPS
    heads = HEADS // GROUPS
    for group in range(GROUPS):

        @pl.loop(0, balls)
        def _(ball):
            backward_heads(
                ball, ball, range(group * heads, (group + 1) * heads), d_att, qkv0, p0, att0, inv0, dqkv
            )

            @pl.when(ball == 1)
            def _():
                if group == 0:
                    advance(*upper)
                else:
                    advance(*upper, sum_o)

        for kind in range(3):
            low = kind * width + group * span_q
            g = nt(h0[...], dqkv[low : low + span_q, :]).astype(BF16)
            if group == 0:
                sum_q.part[:, kind * span_q : (kind + 1) * span_q] = g
            else:
                last[kind].part[...] = g
                advance(last[kind])
        if group == 0:
            advance(sum_q, sum_o)

    advance(*upper, sum_q)

    @pl.loop(0, balls)
    def _(ball):
        d_x[cols(ball), :], gained = backward_norm(
            ball, x[cols(ball), :], gain[0:1], y[cols(ball), :], wqkv.at[0], dqkv
        )
        g_gain[0:1] += gained

        @pl.when(ball == 1)
        def _():
            advance(sum_o, sum_q, *last)

    store(d_x, points_out.at[0])
    small.send(g_gain[...])
    for step in range(8):
        advance(*sums)
        if small.done < 3:
            small.send(small.receive())
    g_gain[...] = small.receive()
    store(g_gain.at[0:2], gain_out)
    store(upper[0].total, qkv_out.at[1, :, : 2 * width])
    store(upper[1].total.at[:, :width], qkv_out.at[1, :, 2 * width :])
    store(upper[1].total.at[:, width:], out_out.at[1])
    store(sum_o.total, out_out.at[0])
    for kind in range(3):
        low = kind * width
        store(sum_q.total.at[:, kind * span_q : (kind + 1) * span_q], qkv_out.at[0, :, low : low + span_q])
        store(last[kind].total, qkv_out.at[0, :, low + span_q : low + width])
    for copy in stores:
        copy.wait()
    for each in sums:
        each.clear()
    small.clear()

    @pl.loop(0, balls)
    def _(ball):
        for kind in range(4):
            for peer in others:
                transfer(kind, ball, seat, peer).wait_send()


def finish_kernel(mixed, d_x, gain, qkv, out, mixed_out, points_out, gain_out, qkv_out, out_out, *rest):
    mixed_v, d_x_v, gain_v, qkv_v, out_v, qkv_f, out_f, load_sem, store_sem = rest
    rows = BALL
    moves = [(mixed, mixed_v, mixed_v, mixed_out), (d_x, d_x_v, d_x_v, points_out), (gain, gain_v, gain_v, gain_out)]
    for layer in range(qkv.shape[0]):
        for low in range(0, qkv.shape[1], rows):
            at = (layer, pl.ds(low, rows))
            moves.append((qkv.at[at], qkv_v.at[at], qkv_f.at[at], qkv_out.at[at]))
            moves.append((out.at[at], out_v.at[at], out_f.at[at], out_out.at[at]))
    moves = moves[3:] + moves[:3]
    loads = [pltpu.make_async_copy(m[0], m[1], load_sem.at[i]) for i, m in enumerate(moves)]
    stores = [pltpu.make_async_copy(m[2], m[3], store_sem.at[i]) for i, m in enumerate(moves)]
    for copy in loads:
        copy.start()
    for load, store, (_, held, ready, _) in zip(loads, stores, moves):
        load.wait()
        if held is not ready:
            ready[...] = held[...].astype(F32)
        store.start()
    for copy in stores:
        copy.wait()


def local(points, ball_lists, gains, w_qkv, w_out, cotangent):
    groups = lax.axis_size("seq")
    rows, width = points.shape[1:]
    balls = rows // BALL
    any_place = pl.BlockSpec(memory_space=pl.ANY)

    def saved(keep):
        return [
            pltpu.VMEM((width, rows), BF16),
            pltpu.VMEM((3 * width, rows), BF16),
            pltpu.VMEM((keep, HEADS, BALL, BALL), BF16),
            pltpu.VMEM((width, rows), BF16),
            pltpu.VMEM((keep, HEADS, BALL), F32),
        ]

    token = pltpu.VMEM((rows, width), BF16)

    def sums(columns):
        shapes = [(width, columns), (width, columns), (1, width // 2, columns)]
        shapes += [(4, width // 8, columns), (4, width // 32, columns), (4, width // 32, columns)]
        return [pltpu.VMEM(shape, BF16) for shape in shapes]

    parts = pl.pallas_call(
        kernel,
        out_shape=[
            jax.ShapeDtypeStruct(points.shape, BF16),
            jax.ShapeDtypeStruct(points.shape, BF16),
            jax.ShapeDtypeStruct(gains.shape, F32),
            jax.ShapeDtypeStruct(w_qkv.shape, BF16),
            jax.ShapeDtypeStruct(w_out.shape, BF16),
        ],
        in_specs=[any_place] * 6,
        out_specs=[any_place] * 5,
        scratch_shapes=[
            pltpu.VMEM((1, rows), jnp.int32),
            token,
            token,
            pltpu.VMEM(gains.shape, F32),
            pltpu.VMEM(w_qkv.shape, BF16),
            pltpu.VMEM(w_out.shape, BF16),
            pltpu.VMEM((2, 3 * width, width), BF16),
            pltpu.VMEM((rows, rows), BF16),
            token,
            *saved(balls),
            *saved(1),
            pltpu.VMEM((3 * width, rows), BF16),
            pltpu.VMEM((width, rows), BF16),
            pltpu.VMEM((4, rows, width), BF16),
            pltpu.VMEM((4, rows, width), BF16),
            token,
            pltpu.VMEM((8, width), F32),
            *[box for columns, _ in SUMS for box in sums(columns)],
            pltpu.VMEM((4, 4, 8, width), F32),
            pltpu.SemaphoreType.DMA((8,)),
            pltpu.SemaphoreType.DMA((16,)),
            pltpu.SemaphoreType.DMA((4, groups)),
            pltpu.SemaphoreType.DMA((4, groups)),
            pltpu.SemaphoreType.DMA((len(SUMS), SUM_SEMS)),
            pltpu.SemaphoreType.DMA((len(SUMS), SUM_SEMS)),
            pltpu.SemaphoreType.DMA((4, 4)),
            pltpu.SemaphoreType.DMA((4, 4)),
        ],
        compiler_params=pltpu.CompilerParams(
            vmem_limit_bytes=VMEM_BYTES, collective_id=0, has_side_effects=True
        ),
    )(points, ball_lists, gains, w_qkv, w_out, cotangent)
    results = [*parts[:3], *(jax.ShapeDtypeStruct(part.shape, F32) for part in parts[3:])]
    moves = 3 + 4 * width // BALL
    return pl.pallas_call(
        finish_kernel,
        out_shape=[jax.ShapeDtypeStruct(result.shape, result.dtype) for result in results],
        in_specs=[any_place] * 5,
        out_specs=[any_place] * 5,
        scratch_shapes=[
            *[pltpu.VMEM(part.shape, part.dtype) for part in parts],
            *[pltpu.VMEM(part.shape, F32) for part in parts[3:]],
            pltpu.SemaphoreType.DMA((moves,)),
            pltpu.SemaphoreType.DMA((moves,)),
        ],
        compiler_params=pltpu.CompilerParams(vmem_limit_bytes=VMEM_BYTES),
    )(*parts)


def solution(mesh):
    return jax.shard_map(
        local,
        mesh=mesh,
        in_specs=(P("dp", "seq", None), P("dp", "seq"), P(), P(), P(), P("dp", "seq", None)),
        out_specs=(P("dp", "seq", None), P("dp", "seq", None), P(), P(), P()),
        check_vma=False,
    )
```

time: 280 us -> 131 us (0.47)
  waiting for transfers between devices: 96.5 us -> 0 us
  blocking collectives: 66.3 us -> 0 us
  Pallas kernels: 92.5 us -> 130 us
  between operations: 14.1 us -> 0.8 us
  local copies, waits for them, and re-layouts: 9.98 us -> 0 us
    psum x1 -> x0, waiting for transfers between devices: 96.5 us -> none  [local(): totals = lax.psum(tuple(grads), ('dp', 'seq'))]
    psum x1 -> x0, blocking collectives: 66.3 us -> none  [local(): totals = lax.psum(tuple(grads), ('dp', 'seq'))]
    pallas_call x1, Pallas kernels: 92.5 us -> 125 us  [local(): pl.pallas_call(kernel, out_shape=[jax.ShapeDtypeStruct(points.shape, BF16...]
    unnamed x12 -> x0, local copies, waits for them, and re-layouts: 9.98 us -> none
    pallas_call x0 -> x1, Pallas kernels: none -> 5.53 us  [local(): pl.pallas_call(finish_kernel, out_shape=[jax.ShapeDtypeStruct(result.shap...]
  transfers between devices with their start and end apart: 1 -> 0, of which waited for: 1 -> 0; matrix products, arithmetic and copies ran while one was open for 0% -> 0% of each run, Pallas kernels for 0% -> 0%
where the time goes in v1:
time: 131 us
  Pallas kernels  130 us (99%)
    pallas_call x1, Pallas kernels, local(): pl.pallas_call(kernel, out_shape=[jax.ShapeDtypeStruct(points.shape, BF16...  125 us
    pallas_call x1, Pallas kernels, local(): pl.pallas_call(finish_kernel, out_shape=[jax.ShapeDtypeStruct(result.shap...  5.53 us

profile of v1, /device:TPU:1, one launch (start us, length us, event | category | flops | bytes accessed | tf_op | source)
XLA Modules:
  0.0 130.9 jit_solution(7932406004592396534)
XLA Ops:
  0.6 124.5 %shard_map.101 = (bf16[1,1024,512]{2,1,0:T(8,128)(2,1)}, bf16[1,1024,512]{2,1,0:T(8,128)(2,1)}, f32[2,512]{1,0:T(2,128)}, bf16[2,512,1536]{2,1,0:T(8,128)(2,1)}, bf16[2,512,512]{2,1,0:T(8,128)(2,1)}) custom-call(bf16[1,1024,512]{2,1,0:T(8,128)(2,1)} %points.1, s32[1,1024]{1,0:T(1,128)} %lists.1, f32[2,512]{1,0:T(2,128)} %gains.1, ...), custom_call_target="tpu_custom_call" | custom-call | tf_op jit(solution)/shard_map/pallas_call | solution.py:574
  125.2 5.5 %shard_map.102 = (bf16[1,1024,512]{2,1,0:T(8,128)(2,1)}, bf16[1,1024,512]{2,1,0:T(8,128)(2,1)}, f32[2,512]{1,0:T(2,128)}, f32[2,512,1536]{2,1,0:T(8,128)}, f32[2,512,512]{2,1,0:T(8,128)}) custom-call(bf16[1,1024,512]{2,1,0:T(8,128)(2,1)} %get-tuple-element.10.mixed, bf16[1,1024,512]{2,1,0:T(8,128)(2,1)} %get-tuple-element.11.d_x, ...), custom_call_target="tpu_custom_call" | custom-call | tf_op jit(solution)/shard_map/pallas_call | solution.py:620

commit v2 on v1

--- a/solution.py
+++ b/solution.py
@@ -69,39 +69,67 @@
     hidden_t = hidden.T
     h_t[:, here] = hidden_t
     qkv_t[:, here] = nn(wqkv_t[...], hidden_t).astype(BF16)
-    for head in range(HEADS):
+
+    def score(head):
         low = head * size
         q = qkv_t[low : low + size, here] * size ** (-0.5)
-        k = qkv_t[width + low : width + low + size, here]
-        v = qkv_t[2 * width + low : 2 * width + low + size, here]
-        scores = tn(k, q)
+        return tn(qkv_t[width + low : width + low + size, here], q)
+
+    def weigh(head, scores):
         weights = jnp.exp(scores - jnp.max(scores, axis=0, keepdims=True))
         share = 1.0 / jnp.sum(weights, axis=0, keepdims=True)
         weights = weights.astype(BF16)
         p_t[keep, head] = weights
         inv[keep, head : head + 1, :] = share
+        return weights, share
+
+    def mix(head, weights, share):
+        low = head * size
+        v = qkv_t[2 * width + low : 2 * width + low + size, here]
         att_t[low : low + size, here] = (nn(v, weights) * share).astype(BF16)
+
+    staggered(range(HEADS), score, weigh, mix)
     return values + tn(att_t[:, here], wout[...])
+
+
+def staggered(heads, *stages):
+    heads = list(heads)
+    held = {}
+    for step in range(len(heads) + len(stages) - 1):
+        for index, stage in enumerate(stages):
+            if 0 <= step - index < len(heads):
+                head = heads[step - index]
+                given = held.pop((head, index), ())
+                result = stage(head, *given)
+                held[head, index + 1] = result if isinstance(result, tuple) else (result,)
 
 
 def backward_heads(ball, keep, heads, d_att, qkv_t, p_t, att_t, inv, dqkv_t):
     width = d_att.shape[0]
     size = width // HEADS
     here = cols(ball)
-    for head in heads:
+
+    def weigh(head):
+        low = head * size
+        v = qkv_t[2 * width + low : 2 * width + low + size, here]
+        d_out = d_att[low : low + size, here].astype(F32) * inv[keep, head : head + 1, :]
+        delta = jnp.sum(d_out * att_t[low : low + size, here].astype(F32), axis=0, keepdims=True)
+        d_out = d_out.astype(BF16)
+        return d_out, delta, tn(v, d_out)
+
+    def score(head, d_out, delta, d_weights):
+        weights = p_t[keep, head]
+        return d_out, weights, (weights.astype(F32) * (d_weights - delta)).astype(BF16)
+
+    def spread(head, d_out, weights, d_scores):
         low = head * size
         q = qkv_t[low : low + size, here] * size ** (-0.5)
         k = qkv_t[width + low : width + low + size, here]
-        v = qkv_t[2 * width + low : 2 * width + low + size, here]
-        share = inv[keep, head : head + 1, :]
-        d_out = d_att[low : low + size, here].astype(F32) * share
-        delta = jnp.sum(d_out * att_t[low : low + size, here].astype(F32), axis=0, keepdims=True)
-        d_out = d_out.astype(BF16)
-        weights = p_t[keep, head]
-        d_scores = (weights.astype(F32) * (tn(v, d_out) - delta)).astype(BF16)
         dqkv_t[low : low + size, here] = (nn(k, d_scores) * size ** (-0.5)).astype(BF16)
         dqkv_t[width + low : width + low + size, here] = nt(q, d_scores).astype(BF16)
         dqkv_t[2 * width + low : 2 * width + low + size, here] = nt(d_out, weights).astype(BF16)
+
+    staggered(heads, weigh, score, spread)
 
 
 def backward_norm(ball, x, gain, dy, wqkv, dqkv_t):
@@ -273,10 +301,10 @@
 SUMS = (
     (1024, ("x", "z", "y")),
     (1024, ("z", "x", "y")),
-    (512, ("z", "x", "y")),
-    (768, ("x", "z", "y")),
-    (256, ("x", "z", "y")),
-    (256, ("z", "y", "x")),
+    (512, ("x", "z", "y")),
+    (768, ("z", "x", "y")),
+    (256, ("x", "y", "z")),
+    (256, ("y", "z", "x")),
     (256, ("y", "x", "z")),
 )
 
@@ -403,7 +431,6 @@
         sent[BACK_R, cols(ball), :] = forward_ball(
             ball, 0, rows_x, gain[1:2], wqkv_t.at[1], wout.at[1], h1, qkv1, p1, att1, inv1
         ).astype(BF16)
-        send(BACK_R, ball)
         arrive(TO_COT, ball)
         d_r = got[TO_COT, cols(ball), :]
         d_att[:, cols(ball)] = nt(wout[1], d_r).astype(BF16)
@@ -414,6 +441,10 @@
         send(BACK_D, ball)
         g_gain[1:2] += gained
 
+    @pl.loop(0, balls)
+    def _(ball):
+        send(BACK_R, ball)
+
     stores = []
 
     def store(source, target):
@@ -436,17 +467,6 @@
 
     @pl.loop(0, balls)
     def _(ball):
-        arrive(BACK_R, ball)
-
-    @pl.loop(0, balls)
-    def _(ball):
-        cot[cols(ball), :] = nn(one_hot_to_tree(order, ball * BALL, BALL), got[BACK_R]).astype(BF16)
-
-    store(cot, mixed_out.at[0])
-    advance(*upper)
-
-    @pl.loop(0, balls)
-    def _(ball):
         arrive(BACK_D, ball)
 
     @pl.loop(0, balls)
@@ -454,6 +474,7 @@
         y[cols(ball), :] = nn(one_hot_to_tree(order, ball * BALL, BALL), got[BACK_D]).astype(BF16)
         d_att[:, cols(ball)] = nt(wout[0], y[cols(ball), :]).astype(BF16)
 
+    advance(*upper)
     sum_o.part[...] = nn(att0[...], y[...]).astype(BF16)
     advance(sum_o)
     span_q = width // GROUPS
@@ -466,12 +487,11 @@
                 ball, ball, range(group * heads, (group + 1) * heads), d_att, qkv0, p0, att0, inv0, dqkv
             )
 
-            @pl.when(ball == 1)
-            def _():
-                if group == 0:
+            if group == 1:
+
+                @pl.when(ball == 2)
+                def _():
                     advance(*upper)
-                else:
-                    advance(*upper, sum_o)
 
         for kind in range(3):
             low = kind * width + group * span_q
@@ -484,7 +504,7 @@
         if group == 0:
             advance(sum_q, sum_o)
 
-    advance(*upper, sum_q)
+    advance(sum_q, *upper)
 
     @pl.loop(0, balls)
     def _(ball):
@@ -493,12 +513,31 @@
         )
         g_gain[0:1] += gained
 
+        @pl.when(ball == 0)
+        def _():
+            advance(sum_o)
+
         @pl.when(ball == 1)
         def _():
-            advance(sum_o, sum_q, *last)
-
+            advance(*upper, *last)
+
+        @pl.when(ball == 2)
+        def _():
+            advance(sum_q, sum_o)
+
+    small.send(g_gain[...])
+    advance(*upper)
     store(d_x, points_out.at[0])
-    small.send(g_gain[...])
+
+    @pl.loop(0, balls)
+    def _(ball):
+        arrive(BACK_R, ball)
+
+    @pl.loop(0, balls)
+    def _(ball):
+        cot[cols(ball), :] = nn(one_hot_to_tree(order, ball * BALL, BALL), got[BACK_R]).astype(BF16)
+
+    store(cot, mixed_out.at[0])
     for step in range(8):
         advance(*sums)
         if small.done < 3:

time: 131 us -> 114 us (0.87)
  Pallas kernels: 130 us -> 113 us
    pallas_call x1, Pallas kernels: 125 us -> 108 us  [local(): pl.pallas_call(kernel, out_shape=[jax.ShapeDtypeStruct(points.shape, BF16...]
where the time goes in v2:
time: 114 us
  Pallas kernels  113 us (99%)
    pallas_call x1, Pallas kernels, local(): pl.pallas_call(kernel, out_shape=[jax.ShapeDtypeStruct(points.shape, BF16...  108 us
    pallas_call x1, Pallas kernels, local(): pl.pallas_call(finish_kernel, out_shape=[jax.ShapeDtypeStruct(result.shap...  5.53 us

profile of v2, /device:TPU:1, one launch (start us, length us, event | category | flops | bytes accessed | tf_op | source)
XLA Modules:
  0.0 114.0 jit_solution(3756853465928199077)
XLA Ops:
  0.6 107.7 %shard_map.101 = (bf16[1,1024,512]{2,1,0:T(8,128)(2,1)}, bf16[1,1024,512]{2,1,0:T(8,128)(2,1)}, f32[2,512]{1,0:T(2,128)}, bf16[2,512,1536]{2,1,0:T(8,128)(2,1)}, bf16[2,512,512]{2,1,0:T(8,128)(2,1)}) custom-call(bf16[1,1024,512]{2,1,0:T(8,128)(2,1)} %points.1, s32[1,1024]{1,0:T(1,128)} %lists.1, f32[2,512]{1,0:T(2,128)} %gains.1, ...), custom_call_target="tpu_custom_call" | custom-call | tf_op jit(solution)/shard_map/pallas_call | solution.py:613
  108.3 5.5 %shard_map.102 = (bf16[1,1024,512]{2,1,0:T(8,128)(2,1)}, bf16[1,1024,512]{2,1,0:T(8,128)(2,1)}, f32[2,512]{1,0:T(2,128)}, f32[2,512,1536]{2,1,0:T(8,128)}, f32[2,512,512]{2,1,0:T(8,128)}) custom-call(bf16[1,1024,512]{2,1,0:T(8,128)(2,1)} %get-tuple-element.10.mixed, bf16[1,1024,512]{2,1,0:T(8,128)(2,1)} %get-tuple-element.11.d_x, ...), custom_call_target="tpu_custom_call" | custom-call | tf_op jit(solution)/shard_map/pallas_call | solution.py:659

commit v3 on v2

--- a/solution.py
+++ b/solution.py
@@ -30,8 +30,8 @@
     return dot(a, b, 0, 0)
 
 
-def cols(ball):
-    return pl.ds(pl.multiple_of(ball * BALL, BALL), BALL)
+def cols(ball, count=1):
+    return pl.ds(pl.multiple_of(ball * BALL, BALL), count * BALL)
 
 
 def norm_scale(x):
@@ -60,35 +60,38 @@
         wqkv_t[low : low + BALL, :] = nt(unit, wqkv[:, low : low + BALL]).astype(BF16)
 
 
-def forward_ball(ball, keep, x, gain, wqkv_t, wout, h_t, qkv_t, p_t, att_t, inv):
+def forward_balls(ball, count, keep, x, gain, wqkv_t, wout, h_t, qkv_t, p_t, att_t, inv):
     width = x.shape[1]
     size = width // HEADS
-    here = cols(ball)
+    here = cols(ball, count)
     values = x.astype(F32)
     hidden = (values * norm_scale(values) * gain).astype(BF16)
     hidden_t = hidden.T
     h_t[:, here] = hidden_t
     qkv_t[:, here] = nn(wqkv_t[...], hidden_t).astype(BF16)
 
-    def score(head):
+    def score(item):
+        nth, head = item
         low = head * size
-        q = qkv_t[low : low + size, here] * size ** (-0.5)
-        return tn(qkv_t[width + low : width + low + size, here], q)
-
-    def weigh(head, scores):
+        q = qkv_t[low : low + size, cols(ball + nth)] * size ** (-0.5)
+        return tn(qkv_t[width + low : width + low + size, cols(ball + nth)], q)
+
+    def weigh(item, scores):
+        nth, head = item
         weights = jnp.exp(scores - jnp.max(scores, axis=0, keepdims=True))
         share = 1.0 / jnp.sum(weights, axis=0, keepdims=True)
         weights = weights.astype(BF16)
-        p_t[keep, head] = weights
-        inv[keep, head : head + 1, :] = share
+        p_t[keep + nth, head] = weights
+        inv[keep + nth, head : head + 1, :] = share
         return weights, share
 
-    def mix(head, weights, share):
+    def mix(item, weights, share):
+        nth, head = item
         low = head * size
-        v = qkv_t[2 * width + low : 2 * width + low + size, here]
-        att_t[low : low + size, here] = (nn(v, weights) * share).astype(BF16)
-
-    staggered(range(HEADS), score, weigh, mix)
+        v = qkv_t[2 * width + low : 2 * width + low + size, cols(ball + nth)]
+        att_t[low : low + size, cols(ball + nth)] = (nn(v, weights) * share).astype(BF16)
+
+    staggered([(nth, head) for nth in range(count) for head in range(HEADS)], score, weigh, mix)
     return values + tn(att_t[:, here], wout[...])
 
 
@@ -132,8 +135,8 @@
     staggered(heads, weigh, score, spread)
 
 
-def backward_norm(ball, x, gain, dy, wqkv, dqkv_t):
-    d_h = nn(wqkv[...], dqkv_t[:, cols(ball)]).T
+def backward_norm(ball, count, x, gain, dy, wqkv, dqkv_t):
+    d_h = nn(wqkv[...], dqkv_t[:, cols(ball, count)]).T
     values = x.astype(F32)
     scale = norm_scale(values)
     unit = values * scale
@@ -151,108 +154,165 @@
         self.peers = {
             axis: [(self.at[axis] + step) % size for step in range(1, size)] for axis, size in sizes.items()
         }
+        self.devices = {
+            axis: [(peer, self.other(axis, peer)) for peer in peers] for axis, peers in self.peers.items()
+        }
+
+    def device(self, axis, peer):
+        for known, device in self.devices[axis]:
+            if known is peer:
+                return device
+        return self.other(axis, peer)
 
     def other(self, axis, value):
         at = {**self.at, axis: value}
         return {"dp": at["y"] // 2 * 4 + at["z"], "seq": at["x"] * 4 + at["y"] % 2 * 2 + at["core"]}
 
 
-SCATTER = (0, 2, 6)
-LAST = 10
-GATHER = (22, 18, 14)
-SUM_SEMS = 24
+HALVES, TURN, PASS, SPREAD, LAST, COLLECT, SHARE, RELAY, BACK = range(9)
 
 
 class Sum:
-    def __init__(self, place, slot, axes, part, total, halves, quarters, pieces, lasts, send_sem, recv_sem):
+    def __init__(self, place, slot, axes, part, total, halves, turns, quarters, pieces, lasts, send_sem, recv_sem):
         self.place, self.slot, self.axes = place, slot, axes
         self.part, self.total = part, total
-        self.inboxes, self.lasts = [halves, quarters, pieces], lasts
+        self.halves, self.turns, self.quarters, self.pieces, self.lasts = halves, turns, quarters, pieces, lasts
         self.send_sem, self.recv_sem = send_sem, recv_sem
-        rows = part.shape[0]
+        rows, columns = part.shape
         self.sizes = [rows, rows // 2, rows // 8, rows // 32]
-        self.names = ["core", axes[0], axes[1]]
         base, self.bases = 0, [0]
-        for size, name in zip(self.sizes[1:], self.names):
+        for size, name in zip(self.sizes[1:], ("core", *axes)):
             base = base + place.at[name] * size
             self.bases.append(base)
+        self.right, self.far, self.left = place.peers[axes[0]]
+        self.sides = (pl.ds(0, columns // 2), pl.ds(columns // 2, columns // 2))
         self.done = 0
 
     def span(self, level, coordinate=None):
         base = self.bases[level] if coordinate is None else self.bases[level - 1] + coordinate * self.sizes[level]
         return pl.ds(pl.multiple_of(base, 16), self.sizes[level])
 
-    def hop(self, first, axis, source, target, here, there):
+    def copy(self, source, target, send, recv, axis, peer):
         return pltpu.make_async_remote_copy(
             src_ref=source,
             dst_ref=target,
-            send_sem=self.send_sem.at[self.slot, first + there],
-            recv_sem=self.recv_sem.at[self.slot, first + here],
-            device_id=self.place.other(axis, there),
+            send_sem=self.send_sem.at[self.slot, send],
+            recv_sem=self.recv_sem.at[self.slot, recv],
+            device_id=self.place.device(axis, peer),
             device_id_type=MESH,
         )
 
-    def scatter(self, level, here, there):
-        axis = self.names[level - 1]
-        inbox = self.inboxes[level - 1].at[0 if level == 1 else here]
-        return self.hop(SCATTER[level - 1], axis, self.part.at[self.span(level, there), :], inbox, here, there)
-
-    def exchange(self, here, there):
-        return self.hop(LAST, self.axes[2], self.lasts.at[here], self.lasts.at[here], here, there)
-
-    def gather(self, level, here, there):
-        rows = self.total.at[self.span(level, here), :]
-        return self.hop(GATHER[level - 1], self.names[level - 1], rows, rows, here, there)
-
-    def start(self, kind, axis, *level):
+    def partner(self, kind):
+        peer = self.place.peers["core"][0]
+        if kind == HALVES:
+            return self.copy(self.part.at[self.span(1, peer), :], self.halves, 0, kind, "core", peer)
+        rows = self.total.at[self.span(1), :]
+        return self.copy(rows, rows, 0, kind, "core", peer)
+
+    def around(self, kind, way):
+        peer = (self.right, self.left)[way]
+        other = (self.left, self.right)[way]
+        side = self.sides[way]
+        if kind == TURN:
+            source, target = self.part.at[self.span(2, self.far), side], self.turns.at[way]
+        elif kind == PASS:
+            source, target = self.part.at[self.span(2, peer), :], self.quarters.at[way]
+        elif kind == SHARE:
+            source = target = self.total.at[self.span(2), :]
+        else:
+            source = target = self.total.at[self.span(2, other), side]
+        return self.copy(source, target, 1, kind, self.axes[0], peer)
+
+    def along(self, kind, here, there):
+        axis = self.axes[2] if kind == LAST else self.axes[1]
+        if kind == SPREAD:
+            source, target = self.part.at[self.span(3, there), :], self.pieces.at[here]
+        elif kind == LAST:
+            source = target = self.lasts.at[here]
+        else:
+            source = target = self.total.at[self.span(3, here), :]
+        return self.copy(source, target, 2, kind, axis, there)
+
+    def start_around(self, kind):
+        for way in range(2):
+            self.around(kind, way).start()
+
+    def start_along(self, kind):
+        axis = self.axes[2] if kind == LAST else self.axes[1]
         for peer in self.place.peers[axis]:
-            kind(*level, self.place.at[axis], peer).start()
-
-    def arrive(self, kind, axis, *level):
-        for peer in self.place.peers[axis]:
-            kind(*level, peer, self.place.at[axis]).wait_recv()
-
-    def left(self, kind, axis, *level):
-        for peer in self.place.peers[axis]:
-            kind(*level, self.place.at[axis], peer).wait_send()
-
-    def added(self, level):
-        axis = self.names[level - 1]
-        self.arrive(self.scatter, axis, level)
-        value = self.part[self.span(level), :].astype(F32)
-        for peer in self.place.peers[axis]:
-            value += self.inboxes[level - 1][0 if level == 1 else peer].astype(F32)
+            self.along(kind, self.place.at[axis], peer).start()
+
+    def arrive(self, kind):
+        rows = self.part.shape[0]
+        eighth, last = rows // 8, rows // 32
+        held = {
+            HALVES: self.halves,
+            TURN: self.turns,
+            PASS: self.quarters,
+            SPREAD: self.pieces.at[pl.ds(0, 3)],
+            LAST: self.lasts.at[pl.ds(0, 3)],
+            COLLECT: self.total.at[pl.ds(0, 3 * last), :],
+            SHARE: self.total.at[pl.ds(0, 2 * eighth), :],
+            RELAY: self.total.at[pl.ds(0, eighth), :],
+            BACK: self.total.at[pl.ds(0, rows // 2), :],
+        }[kind]
+        pltpu.make_async_copy(held, held, self.recv_sem.at[self.slot, kind]).wait()
+
+    def add(self, rows, side, *arrived):
+        value = self.part[rows, side].astype(F32)
+        for each in arrived:
+            value += each.astype(F32)
         return value.astype(BF16)
 
     def step(self):
         step, self.done = self.done, self.done + 1
-        last = self.axes[2]
+        everything = pl.ds(0, self.part.shape[1])
         if step == 0:
-            self.start(self.scatter, self.names[0], 1)
-        elif step in (1, 2):
-            self.part[self.span(step), :] = self.added(step)
-            self.start(self.scatter, self.names[step], step + 1)
+            self.partner(HALVES).start()
+        elif step == 1:
+            self.arrive(HALVES)
+            self.part[self.span(1), :] = self.add(self.span(1), everything, self.halves[...])
+            self.start_around(TURN)
+        elif step == 2:
+            self.arrive(TURN)
+            for way, peer in enumerate((self.right, self.left)):
+                rows, side = self.span(2, peer), self.sides[way]
+                self.part[rows, side] = self.add(rows, side, self.turns[way])
+            self.start_around(PASS)
         elif step == 3:
-            self.lasts[self.place.at[last]] = self.added(3)
-            self.start(self.exchange, last)
+            self.arrive(PASS)
+            self.part[self.span(2), :] = self.add(self.span(2), everything, self.quarters[0], self.quarters[1])
+            self.start_along(SPREAD)
         elif step == 4:
-            self.arrive(self.exchange, last)
+            self.arrive(SPREAD)
+            mine = self.place.at[self.axes[2]]
+            peers = self.place.peers[self.axes[1]]
+            self.lasts[mine] = self.add(self.span(3), everything, *[self.pieces[peer] for peer in peers])
+            self.start_along(LAST)
+        elif step == 5:
+            self.arrive(LAST)
             value = self.lasts[0].astype(F32)
             for peer in range(1, 4):
                 value += self.lasts[peer].astype(F32)
             self.total[self.span(3), :] = value.astype(BF16)
-            self.start(self.gather, self.names[2], 3)
-        elif step in (5, 6):
-            self.arrive(self.gather, self.names[7 - step], 8 - step)
-            self.start(self.gather, self.names[6 - step], 7 - step)
+            self.start_along(COLLECT)
+        elif step == 6:
+            self.arrive(COLLECT)
+            self.start_around(SHARE)
         elif step == 7:
-            self.arrive(self.gather, self.names[0], 1)
+            self.arrive(SHARE)
+            self.start_around(RELAY)
+        elif step == 8:
+            self.arrive(RELAY)
+            self.partner(BACK).start()
+        elif step == 9:
+            self.arrive(BACK)
 
     def clear(self):
-        for level in (1, 2, 3):
-            self.left(self.scatter, self.names[level - 1], level)
-            self.left(self.gather, self.names[level - 1], level)
-        self.left(self.exchange, self.axes[2])
+        rows = self.part.shape[0]
+        for index, sent in enumerate((rows, 6 * rows // 8, 9 * rows // 32)):
+            held = self.part.at[pl.ds(0, sent), :]
+            pltpu.make_async_copy(held, held, self.send_sem.at[self.slot, index]).wait()
 
 
 class SmallSum:
@@ -267,9 +327,9 @@
         return pltpu.make_async_remote_copy(
             src_ref=box,
             dst_ref=box,
-            send_sem=self.send_sem.at[step, there],
-            recv_sem=self.recv_sem.at[step, here],
-            device_id=self.place.other(self.axes[step], there),
+            send_sem=self.send_sem.at[step],
+            recv_sem=self.recv_sem.at[step],
+            device_id=self.place.device(self.axes[step], there),
             device_id_type=MESH,
         )
 
@@ -282,29 +342,32 @@
 
     def receive(self):
         axis = self.axes[self.done]
-        for peer in self.place.peers[axis]:
-            self.hop(self.done, peer, self.place.at[axis]).wait_recv()
+        self.wait(self.done, self.recv_sem)
         value = self.boxes[self.done, 0]
         for peer in range(1, len(self.place.peers[axis]) + 1):
             value += self.boxes[self.done, peer]
         self.done += 1
         return value
 
+    def wait(self, step, sem):
+        held = self.boxes.at[step, pl.ds(0, len(self.place.peers[self.axes[step]]))]
+        pltpu.make_async_copy(held, held, sem.at[step]).wait()
+
     def clear(self):
-        for step, axis in enumerate(self.axes):
-            for peer in self.place.peers[axis]:
-                self.hop(step, self.place.at[axis], peer).wait_send()
+        for step in range(len(self.axes)):
+            self.wait(step, self.send_sem)
 
 
 TO_X, TO_COT, BACK_R, BACK_D = range(4)
 GROUPS = 2
+PAIR = 2
 SUMS = (
     (1024, ("x", "z", "y")),
     (1024, ("z", "x", "y")),
     (512, ("x", "z", "y")),
     (768, ("z", "x", "y")),
     (256, ("x", "y", "z")),
-    (256, ("y", "z", "x")),
+    (256, ("z", "y", "x")),
     (256, ("y", "x", "z")),
 )
 
@@ -316,7 +379,7 @@
     h0, qkv0, p0, att0, inv0, h1, qkv1, p1, att1, inv1, dqkv, d_att,
     sent, got, d_x, g_gain, *rest,
 ):
-    sum_boxes, rest = rest[: 6 * len(SUMS)], rest[6 * len(SUMS) :]
+    sum_boxes, rest = rest[: 7 * len(SUMS)], rest[7 * len(SUMS) :]
     boxes, load_sem, store_sem, send_sem, recv_sem, sum_send, sum_recv, small_send, small_recv = rest
     groups = lax.axis_size("seq")
     me = lax.axis_index("seq")
@@ -328,7 +391,7 @@
     seat = me % near
     place = Place()
     sums = [
-        Sum(place, slot, axes, *sum_boxes[6 * slot : 6 * slot + 6], sum_send, sum_recv)
+        Sum(place, slot, axes, *sum_boxes[7 * slot : 7 * slot + 7], sum_send, sum_recv)
         for slot, (columns, axes) in enumerate(SUMS)
     ]
     upper, sum_o, sum_q, last = sums[0:2], sums[2], sums[3], sums[4:7]
@@ -369,8 +432,8 @@
         return pltpu.make_async_remote_copy(
             src_ref=sent.at[kind, span(ball * near + there), :],
             dst_ref=got.at[kind, span(ball * near + here), :],
-            send_sem=send_sem.at[kind, ball * near + there],
-            recv_sem=recv_sem.at[kind, ball * near + here],
+            send_sem=send_sem.at[kind],
+            recv_sem=recv_sem.at[kind, ball],
             device_id={"seq": home * near + there},
             device_id_type=MESH,
         )
@@ -382,11 +445,11 @@
         got[kind, own, :] = sent[kind, own, :]
 
     def arrive(kind, ball):
-        for peer in others:
-            transfer(kind, ball, peer, seat).wait_recv()
-
-    def gather(kind, source, group):
-        sent[kind, cols(group), :] = nn(onto[cols(group), :], source[...]).astype(BF16)
+        held = got.at[kind, pl.ds(0, (near - 1) * block), :]
+        pltpu.make_async_copy(held, held, recv_sem.at[kind, ball]).wait()
+
+    def gather(kind, source, ball):
+        sent[kind, cols(ball, PAIR), :] = nn(onto[cols(ball, PAIR), :], source[...]).astype(BF16)
 
     lists_in.wait()
 
@@ -398,26 +461,29 @@
     cot_in.wait()
     pl.semaphore_wait(barrier, near - 1 + 8)
 
-    @pl.loop(0, balls)
+    @pl.loop(0, balls, step=PAIR)
     def _(ball):
         gather(TO_COT, cot, ball)
-        send(TO_COT, ball)
+        for nth in range(PAIR):
+            send(TO_COT, ball + nth)
 
     x_in.wait()
     for copy in small_in:
         copy.wait()
     transpose_by_unit(wqkv.at[0], wqkv_t.at[0])
 
-    @pl.loop(0, balls)
-    def _(ball):
-        y[cols(ball), :] = forward_ball(
-            ball, ball, x[cols(ball), :], gain[0:1], wqkv_t.at[0], wout.at[0], h0, qkv0, p0, att0, inv0
+    @pl.loop(0, balls, step=PAIR)
+    def _(ball):
+        here = cols(ball, PAIR)
+        y[here, :] = forward_balls(
+            ball, PAIR, ball, x[here, :], gain[0:1], wqkv_t.at[0], wout.at[0], h0, qkv0, p0, att0, inv0
         ).astype(BF16)
 
-    @pl.loop(0, balls)
+    @pl.loop(0, balls, step=PAIR)
     def _(ball):
         gather(TO_X, y, ball)
-        send(TO_X, ball)
+        for nth in range(PAIR):
+            send(TO_X, ball + nth)
 
     for copy in late_in:
         copy.wait()
@@ -428,15 +494,15 @@
     def _(ball):
         arrive(TO_X, ball)
         rows_x = got[TO_X, cols(ball), :]
-        sent[BACK_R, cols(ball), :] = forward_ball(
-            ball, 0, rows_x, gain[1:2], wqkv_t.at[1], wout.at[1], h1, qkv1, p1, att1, inv1
+        sent[BACK_R, cols(ball), :] = forward_balls(
+            ball, 1, 0, rows_x, gain[1:2], wqkv_t.at[1], wout.at[1], h1, qkv1, p1, att1, inv1
         ).astype(BF16)
         arrive(TO_COT, ball)
         d_r = got[TO_COT, cols(ball), :]
         d_att[:, cols(ball)] = nt(wout[1], d_r).astype(BF16)
         backward_heads(ball, 0, range(HEADS), d_att, qkv1, p1, att1, inv1, dqkv)
         sent[BACK_D, cols(ball), :], gained = backward_norm(
-            ball, got[TO_X, cols(ball), :], gain[1:2], d_r, wqkv.at[1], dqkv
+            ball, 1, got[TO_X, cols(ball), :], gain[1:2], d_r, wqkv.at[1], dqkv
         )
         send(BACK_D, ball)
         g_gain[1:2] += gained
@@ -469,12 +535,16 @@
     def _(ball):
         arrive(BACK_D, ball)
 
-    @pl.loop(0, balls)
-    def _(ball):
-        y[cols(ball), :] = nn(one_hot_to_tree(order, ball * BALL, BALL), got[BACK_D]).astype(BF16)
-        d_att[:, cols(ball)] = nt(wout[0], y[cols(ball), :]).astype(BF16)
-
-    advance(*upper)
+    @pl.loop(0, balls, step=PAIR)
+    def _(ball):
+        here = cols(ball, PAIR)
+        y[here, :] = nn(one_hot_to_tree(order, ball * BALL, PAIR * BALL), got[BACK_D]).astype(BF16)
+        d_att[:, here] = nt(wout[0], y[here, :]).astype(BF16)
+
+        @pl.when(ball == 0)
+        def _():
+            advance(*upper)
+
     sum_o.part[...] = nn(att0[...], y[...]).astype(BF16)
     advance(sum_o)
     span_q = width // GROUPS
@@ -487,11 +557,16 @@
                 ball, ball, range(group * heads, (group + 1) * heads), d_att, qkv0, p0, att0, inv0, dqkv
             )
 
-            if group == 1:
-
-                @pl.when(ball == 2)
-                def _():
-                    advance(*upper)
+            @pl.when(ball == 0)
+            def _():
+                advance(*upper)
+
+            @pl.when(ball == 2)
+            def _():
+                if group == 0:
+                    advance(sum_o)
+                else:
+                    advance(sum_q, sum_o)
 
         for kind in range(3):
             low = kind * width + group * span_q
@@ -502,43 +577,42 @@
                 last[kind].part[...] = g
                 advance(last[kind])
         if group == 0:
-            advance(sum_q, sum_o)
-
-    advance(sum_q, *upper)
-
-    @pl.loop(0, balls)
-    def _(ball):
-        d_x[cols(ball), :], gained = backward_norm(
-            ball, x[cols(ball), :], gain[0:1], y[cols(ball), :], wqkv.at[0], dqkv
+            advance(sum_q)
+        else:
+            advance(*upper)
+
+    @pl.loop(0, balls, step=PAIR)
+    def _(ball):
+        here = cols(ball, PAIR)
+        d_x[here, :], gained = backward_norm(
+            ball, PAIR, x[here, :], gain[0:1], y[here, :], wqkv.at[0], dqkv
         )
         g_gain[0:1] += gained
 
         @pl.when(ball == 0)
         def _():
-            advance(sum_o)
-
-        @pl.when(ball == 1)
-        def _():
-            advance(*upper, *last)
-
-        @pl.when(ball == 2)
+            advance(sum_q, sum_o, *upper, *last)
+
+    advance(sum_q, sum_o, *last)
+    small.send(g_gain[...])
+    advance(*upper, *last)
+    store(d_x, points_out.at[0])
+
+    @pl.loop(0, balls)
+    def _(ball):
+        arrive(BACK_R, ball)
+
+    @pl.loop(0, balls, step=PAIR)
+    def _(ball):
+        here = cols(ball, PAIR)
+        cot[here, :] = nn(one_hot_to_tree(order, ball * BALL, PAIR * BALL), got[BACK_R]).astype(BF16)
+
+        @pl.when(ball == 0)
         def _():
             advance(sum_q, sum_o)
 
-    small.send(g_gain[...])
-    advance(*upper)
-    store(d_x, points_out.at[0])
-
-    @pl.loop(0, balls)
-    def _(ball):
-        arrive(BACK_R, ball)
-
-    @pl.loop(0, balls)
-    def _(ball):
-        cot[cols(ball), :] = nn(one_hot_to_tree(order, ball * BALL, BALL), got[BACK_R]).astype(BF16)
-
     store(cot, mixed_out.at[0])
-    for step in range(8):
+    for step in range(10):
         advance(*sums)
         if small.done < 3:
             small.send(small.receive())
@@ -558,11 +632,9 @@
         each.clear()
     small.clear()
 
-    @pl.loop(0, balls)
-    def _(ball):
-        for kind in range(4):
-            for peer in others:
-                transfer(kind, ball, seat, peer).wait_send()
+    for kind in range(4):
+        held = sent.at[kind, pl.ds(0, balls * (near - 1) * block), :]
+        pltpu.make_async_copy(held, held, send_sem.at[kind]).wait()
 
 
 def finish_kernel(mixed, d_x, gain, qkv, out, mixed_out, points_out, gain_out, qkv_out, out_out, *rest):
@@ -606,8 +678,8 @@
     token = pltpu.VMEM((rows, width), BF16)
 
     def sums(columns):
-        shapes = [(width, columns), (width, columns), (1, width // 2, columns)]
-        shapes += [(4, width // 8, columns), (4, width // 32, columns), (4, width // 32, columns)]
+        shapes = [(width, columns), (width, columns), (width // 2, columns), (2, width // 8, columns // 2)]
+        shapes += [(2, width // 8, columns), (4, width // 32, columns), (4, width // 32, columns)]
         return [pltpu.VMEM(shape, BF16) for shape in shapes]
 
     parts = pl.pallas_call(
@@ -643,12 +715,12 @@
             pltpu.VMEM((4, 4, 8, width), F32),
             pltpu.SemaphoreType.DMA((8,)),
             pltpu.SemaphoreType.DMA((16,)),
-            pltpu.SemaphoreType.DMA((4, groups)),
-            pltpu.SemaphoreType.DMA((4, groups)),
-            pltpu.SemaphoreType.DMA((len(SUMS), SUM_SEMS)),
-            pltpu.SemaphoreType.DMA((len(SUMS), SUM_SEMS)),
-            pltpu.SemaphoreType.DMA((4, 4)),
-            pltpu.SemaphoreType.DMA((4, 4)),
+            pltpu.SemaphoreType.DMA((4,)),
+            pltpu.SemaphoreType.DMA((4, balls)),
+            pltpu.SemaphoreType.DMA((len(SUMS), 3)),
+            pltpu.SemaphoreType.DMA((len(SUMS), 9)),
+            pltpu.SemaphoreType.DMA((4,)),
+            pltpu.SemaphoreType.DMA((4,)),
         ],
         compiler_params=pltpu.CompilerParams(
             vmem_limit_bytes=VMEM_BYTES, collective_id=0, has_side_effects=True

time: 114 us -> 109 us (0.956)
  Pallas kernels: 113 us -> 108 us
    pallas_call x1, Pallas kernels: 108 us -> 102 us  [local(): pl.pallas_call(kernel, out_shape=[jax.ShapeDtypeStruct(points.shape, BF16...]
where the time goes in v3:
time: 109 us
  Pallas kernels  108 us (99%)
    pallas_call x1, Pallas kernels, local(): pl.pallas_call(kernel, out_shape=[jax.ShapeDtypeStruct(points.shape, BF16...  102 us
    pallas_call x1, Pallas kernels, local(): pl.pallas_call(finish_kernel, out_shape=[jax.ShapeDtypeStruct(result.shap...  5.53 us

profile of v3, /device:TPU:1, one launch (start us, length us, event | category | flops | bytes accessed | tf_op | source)
XLA Modules:
  0.0 108.5 jit_solution(3087938620525190945)
XLA Ops:
  0.6 102.2 %shard_map.101 = (bf16[1,1024,512]{2,1,0:T(8,128)(2,1)}, bf16[1,1024,512]{2,1,0:T(8,128)(2,1)}, f32[2,512]{1,0:T(2,128)}, bf16[2,512,1536]{2,1,0:T(8,128)(2,1)}, bf16[2,512,512]{2,1,0:T(8,128)(2,1)}) custom-call(bf16[1,1024,512]{2,1,0:T(8,128)(2,1)} %points.1, s32[1,1024]{1,0:T(1,128)} %lists.1, f32[2,512]{1,0:T(2,128)} %gains.1, ...), custom_call_target="tpu_custom_call" | custom-call | tf_op jit(solution)/shard_map/pallas_call | solution.py:685
  102.8 5.5 %shard_map.102 = (bf16[1,1024,512]{2,1,0:T(8,128)(2,1)}, bf16[1,1024,512]{2,1,0:T(8,128)(2,1)}, f32[2,512]{1,0:T(2,128)}, f32[2,512,1536]{2,1,0:T(8,128)}, f32[2,512,512]{2,1,0:T(8,128)}) custom-call(bf16[1,1024,512]{2,1,0:T(8,128)(2,1)} %get-tuple-element.10.mixed, bf16[1,1024,512]{2,1,0:T(8,128)(2,1)} %get-tuple-element.11.d_x, ...), custom_call_target="tpu_custom_call" | custom-call | tf_op jit(solution)/shard_map/pallas_call | solution.py:731

commit v4 on v3

--- a/solution.py
+++ b/solution.py
@@ -169,6 +169,7 @@
         return {"dp": at["y"] // 2 * 4 + at["z"], "seq": at["x"] * 4 + at["y"] % 2 * 2 + at["core"]}
 
 
+STEPS = 10
 HALVES, TURN, PASS, SPREAD, LAST, COLLECT, SHARE, RELAY, BACK = range(9)
 
 
@@ -557,16 +558,9 @@
                 ball, ball, range(group * heads, (group + 1) * heads), d_att, qkv0, p0, att0, inv0, dqkv
             )
 
-            @pl.when(ball == 0)
-            def _():
-                advance(*upper)
-
             @pl.when(ball == 2)
             def _():
-                if group == 0:
-                    advance(sum_o)
-                else:
-                    advance(sum_q, sum_o)
+                advance(sum_o)
 
         for kind in range(3):
             low = kind * width + group * span_q
@@ -576,10 +570,7 @@
             else:
                 last[kind].part[...] = g
                 advance(last[kind])
-        if group == 0:
-            advance(sum_q)
-        else:
-            advance(*upper)
+        advance(*upper, sum_q)
 
     @pl.loop(0, balls, step=PAIR)
     def _(ball):
@@ -591,11 +582,10 @@
 
         @pl.when(ball == 0)
         def _():
-            advance(sum_q, sum_o, *upper, *last)
-
-    advance(sum_q, sum_o, *last)
+            advance(*last, sum_q, sum_o)
+
     small.send(g_gain[...])
-    advance(*upper, *last)
+    advance(*last, sum_q, *upper, sum_o)
     store(d_x, points_out.at[0])
 
     @pl.loop(0, balls)
@@ -609,23 +599,37 @@
 
         @pl.when(ball == 0)
         def _():
-            advance(sum_q, sum_o)
+            advance(*last, sum_q, sum_o, *upper)
 
     store(cot, mixed_out.at[0])
-    for step in range(10):
-        advance(*sums)
+
+    def store_total(each):
+        if each is upper[0]:
+            store(each.total, qkv_out.at[1, :, : 2 * width])
+        elif each is upper[1]:
+            store(each.total.at[:, :width], qkv_out.at[1, :, 2 * width :])
+            store(each.total.at[:, width:], out_out.at[1])
+        elif each is sum_o:
+            store(each.total, out_out.at[0])
+        elif each is sum_q:
+            for kind in range(3):
+                columns = pl.ds(kind * width, span_q)
+                store(each.total.at[:, kind * span_q : (kind + 1) * span_q], qkv_out.at[0, :, columns])
+        else:
+            columns = pl.ds(last.index(each) * width + span_q, span_q)
+            store(each.total, qkv_out.at[0, :, columns])
+
+    while any(each.done < STEPS for each in sums):
+        for each in (*last, sum_q, *upper, sum_o):
+            if each.done < STEPS:
+                each.step()
+                if each.done == STEPS:
+                    store_total(each)
         if small.done < 3:
             small.send(small.receive())
-    g_gain[...] = small.receive()
-    store(g_gain.at[0:2], gain_out)
-    store(upper[0].total, qkv_out.at[1, :, : 2 * width])
-    store(upper[1].total.at[:, :width], qkv_out.at[1, :, 2 * width :])
-    store(upper[1].total.at[:, width:], out_out.at[1])
-    store(sum_o.total, out_out.at[0])
-    for kind in range(3):
-        low = kind * width
-        store(sum_q.total.at[:, kind * span_q : (kind + 1) * span_q], qkv_out.at[0, :, low : low + span_q])
-        store(last[kind].total, qkv_out.at[0, :, low + span_q : low + width])
+        elif small.done == 3:
+            g_gain[...] = small.receive()
+            store(g_gain.at[0:2], gain_out)
     for copy in stores:
         copy.wait()
     for each in sums:

time: 109 us -> 106 us (0.972)
  Pallas kernels: 108 us -> 106 us
    pallas_call x1, Pallas kernels: 102 us -> 100 us  [local(): pl.pallas_call(kernel, out_shape=[jax.ShapeDtypeStruct(points.shape, BF16...]
where the time goes in v4:
time: 106 us
  Pallas kernels  106 us (100%)
    pallas_call x1, Pallas kernels, local(): pl.pallas_call(kernel, out_shape=[jax.ShapeDtypeStruct(points.shape, BF16...  100 us
    pallas_call x1, Pallas kernels, local(): pl.pallas_call(finish_kernel, out_shape=[jax.ShapeDtypeStruct(result.shap...  5.53 us

profile of v4, /device:TPU:1, one launch (start us, length us, event | category | flops | bytes accessed | tf_op | source)
XLA Modules:
  0.0 106.3 jit_solution(15515292486397478512)
XLA Ops:
  0.6 100.0 %shard_map.101 = (bf16[1,1024,512]{2,1,0:T(8,128)(2,1)}, bf16[1,1024,512]{2,1,0:T(8,128)(2,1)}, f32[2,512]{1,0:T(2,128)}, bf16[2,512,1536]{2,1,0:T(8,128)(2,1)}, bf16[2,512,512]{2,1,0:T(8,128)(2,1)}) custom-call(bf16[1,1024,512]{2,1,0:T(8,128)(2,1)} %points.1, s32[1,1024]{1,0:T(1,128)} %lists.1, f32[2,512]{1,0:T(2,128)} %gains.1, ...), custom_call_target="tpu_custom_call" | custom-call | tf_op jit(solution)/shard_map/pallas_call | solution.py:689
  100.6 5.5 %shard_map.102 = (bf16[1,1024,512]{2,1,0:T(8,128)(2,1)}, bf16[1,1024,512]{2,1,0:T(8,128)(2,1)}, f32[2,512]{1,0:T(2,128)}, f32[2,512,1536]{2,1,0:T(8,128)}, f32[2,512,512]{2,1,0:T(8,128)}) custom-call(bf16[1,1024,512]{2,1,0:T(8,128)(2,1)} %get-tuple-element.10.mixed, bf16[1,1024,512]{2,1,0:T(8,128)(2,1)} %get-tuple-element.11.d_x, ...), custom_call_target="tpu_custom_call" | custom-call | tf_op jit(solution)/shard_map/pallas_call | solution.py:735

commit v5 on v4

--- a/solution.py
+++ b/solution.py
@@ -60,7 +60,7 @@
         wqkv_t[low : low + BALL, :] = nt(unit, wqkv[:, low : low + BALL]).astype(BF16)
 
 
-def forward_balls(ball, count, keep, x, gain, wqkv_t, wout, h_t, qkv_t, p_t, att_t, inv):
+def forward_balls(ball, count, keep, x, gain, wqkv_t, h_t, qkv_t, p_t, att_t, inv):
     width = x.shape[1]
     size = width // HEADS
     here = cols(ball, count)
@@ -92,7 +92,10 @@
         att_t[low : low + size, cols(ball + nth)] = (nn(v, weights) * share).astype(BF16)
 
     staggered([(nth, head) for nth in range(count) for head in range(HEADS)], score, weigh, mix)
-    return values + tn(att_t[:, here], wout[...])
+
+
+def project(x, att_t, wout):
+    return (x.astype(F32) + tn(att_t, wout[...])).astype(BF16)
 
 
 def staggered(heads, *stages):
@@ -363,9 +366,9 @@
 GROUPS = 2
 PAIR = 2
 SUMS = (
+    (768, ("x", "z", "y")),
+    (768, ("z", "x", "y")),
     (1024, ("x", "z", "y")),
-    (1024, ("z", "x", "y")),
-    (512, ("x", "z", "y")),
     (768, ("z", "x", "y")),
     (256, ("x", "y", "z")),
     (256, ("z", "y", "x")),
@@ -476,9 +479,8 @@
     @pl.loop(0, balls, step=PAIR)
     def _(ball):
         here = cols(ball, PAIR)
-        y[here, :] = forward_balls(
-            ball, PAIR, ball, x[here, :], gain[0:1], wqkv_t.at[0], wout.at[0], h0, qkv0, p0, att0, inv0
-        ).astype(BF16)
+        forward_balls(ball, PAIR, ball, x[here, :], gain[0:1], wqkv_t.at[0], h0, qkv0, p0, att0, inv0)
+        y[here, :] = project(x[here, :], att0[:, here], wout.at[0])
 
     @pl.loop(0, balls, step=PAIR)
     def _(ball):
@@ -494,10 +496,9 @@
     @pl.loop(0, balls)
     def _(ball):
         arrive(TO_X, ball)
-        rows_x = got[TO_X, cols(ball), :]
-        sent[BACK_R, cols(ball), :] = forward_balls(
-            ball, 1, 0, rows_x, gain[1:2], wqkv_t.at[1], wout.at[1], h1, qkv1, p1, att1, inv1
-        ).astype(BF16)
+        forward_balls(
+            ball, 1, 0, got[TO_X, cols(ball), :], gain[1:2], wqkv_t.at[1], h1, qkv1, p1, att1, inv1
+        )
         arrive(TO_COT, ball)
         d_r = got[TO_COT, cols(ball), :]
         d_att[:, cols(ball)] = nt(wout[1], d_r).astype(BF16)
@@ -508,10 +509,6 @@
         send(BACK_D, ball)
         g_gain[1:2] += gained
 
-    @pl.loop(0, balls)
-    def _(ball):
-        send(BACK_R, ball)
-
     stores = []
 
     def store(source, target):
@@ -521,16 +518,23 @@
         return copy
 
     width = x.shape[1]
-    first, second = upper[0].part, upper[1].part
-    second[:, width:] = nn(att1[...], got[TO_COT]).astype(BF16)
-    first[...] = nt(h1[...], dqkv[: 2 * width, :]).astype(BF16)
-    second[:, :width] = nt(h1[...], dqkv[2 * width :, :]).astype(BF16)
-
     def advance(*which):
         for each in which:
             each.step()
 
-    advance(*upper)
+    half = 3 * width // 2
+    for nth, each in enumerate(upper):
+        each.part[...] = nt(h1[...], dqkv[nth * half : (nth + 1) * half, :]).astype(BF16)
+        advance(each)
+
+    @pl.loop(0, balls, step=PAIR)
+    def _(ball):
+        here = cols(ball, PAIR)
+        sent[BACK_R, here, :] = project(got[TO_X, here, :], att1[:, here], wout.at[1])
+        for nth in range(PAIR):
+            send(BACK_R, ball + nth)
+
+    sum_o.part[:, width:] = nn(att1[...], got[TO_COT]).astype(BF16)
 
     @pl.loop(0, balls)
     def _(ball):
@@ -546,7 +550,7 @@
         def _():
             advance(*upper)
 
-    sum_o.part[...] = nn(att0[...], y[...]).astype(BF16)
+    sum_o.part[:, :width] = nn(att0[...], y[...]).astype(BF16)
     advance(sum_o)
     span_q = width // GROUPS
     heads = HEADS // GROUPS
@@ -604,13 +608,11 @@
     store(cot, mixed_out.at[0])
 
     def store_total(each):
-        if each is upper[0]:
-            store(each.total, qkv_out.at[1, :, : 2 * width])
-        elif each is upper[1]:
-            store(each.total.at[:, :width], qkv_out.at[1, :, 2 * width :])
+        if each in upper:
+            store(each.total, qkv_out.at[1, :, pl.ds(upper.index(each) * half, half)])
+        elif each is sum_o:
+            store(each.total.at[:, :width], out_out.at[0])
             store(each.total.at[:, width:], out_out.at[1])
-        elif each is sum_o:
-            store(each.total, out_out.at[0])
         elif each is sum_q:
             for kind in range(3):
                 columns = pl.ds(kind * width, span_q)

time: 106 us -> 107 us (level)
  no operation moved by 1% of the time
where the time goes in v5:
time: 107 us
  Pallas kernels  106 us (99%)
    pallas_call x1, Pallas kernels, local(): pl.pallas_call(kernel, out_shape=[jax.ShapeDtypeStruct(points.shape, BF16...  100 us
    pallas_call x1, Pallas kernels, local(): pl.pallas_call(finish_kernel, out_shape=[jax.ShapeDtypeStruct(result.shap...  5.53 us

profile of v5, /device:TPU:1, one launch (start us, length us, event | category | flops | bytes accessed | tf_op | source)
XLA Modules:
  0.0 106.5 jit_solution(11097527450900062602)
XLA Ops:
  0.6 100.2 %shard_map.101 = (bf16[1,1024,512]{2,1,0:T(8,128)(2,1)}, bf16[1,1024,512]{2,1,0:T(8,128)(2,1)}, f32[2,512]{1,0:T(2,128)}, bf16[2,512,1536]{2,1,0:T(8,128)(2,1)}, bf16[2,512,512]{2,1,0:T(8,128)(2,1)}) custom-call(bf16[1,1024,512]{2,1,0:T(8,128)(2,1)} %points.1, s32[1,1024]{1,0:T(1,128)} %lists.1, f32[2,512]{1,0:T(2,128)} %gains.1, ...), custom_call_target="tpu_custom_call" | custom-call | tf_op jit(solution)/shard_map/pallas_call | solution.py:691
  100.8 5.5 %shard_map.102 = (bf16[1,1024,512]{2,1,0:T(8,128)(2,1)}, bf16[1,1024,512]{2,1,0:T(8,128)(2,1)}, f32[2,512]{1,0:T(2,128)}, f32[2,512,1536]{2,1,0:T(8,128)}, f32[2,512,512]{2,1,0:T(8,128)}) custom-call(bf16[1,1024,512]{2,1,0:T(8,128)(2,1)} %get-tuple-element.10.mixed, bf16[1,1024,512]{2,1,0:T(8,128)(2,1)} %get-tuple-element.11.d_x, ...), custom_call_target="tpu_custom_call" | custom-call | tf_op jit(solution)/shard_map/pallas_call | solution.py:737

commit v6 on v5

--- a/solution.py
+++ b/solution.py
@@ -365,6 +365,7 @@
 TO_X, TO_COT, BACK_R, BACK_D = range(4)
 GROUPS = 2
 PAIR = 2
+MIXED_TURNS = (3, 4)
 SUMS = (
     (768, ("x", "z", "y")),
     (768, ("z", "x", "y")),
@@ -465,11 +466,11 @@
     cot_in.wait()
     pl.semaphore_wait(barrier, near - 1 + 8)
 
-    @pl.loop(0, balls, step=PAIR)
-    def _(ball):
+    for ball in range(0, balls, PAIR):
         gather(TO_COT, cot, ball)
         for nth in range(PAIR):
-            send(TO_COT, ball + nth)
+            if ball + nth < balls - 1:
+                send(TO_COT, ball + nth)
 
     x_in.wait()
     for copy in small_in:
@@ -488,25 +489,29 @@
         for nth in range(PAIR):
             send(TO_X, ball + nth)
 
+    send(TO_COT, balls - 1)
+
     for copy in late_in:
         copy.wait()
     transpose_by_unit(wqkv.at[1], wqkv_t.at[1])
     g_gain[...] = jnp.zeros_like(g_gain)
 
-    @pl.loop(0, balls)
-    def _(ball):
-        arrive(TO_X, ball)
-        forward_balls(
-            ball, 1, 0, got[TO_X, cols(ball), :], gain[1:2], wqkv_t.at[1], h1, qkv1, p1, att1, inv1
+    for ball, count in ((0, 1), (1, balls - 2), (balls - 1, 1)):
+        here = cols(ball, count)
+        for nth in range(count):
+            arrive(TO_X, ball + nth)
+        forward_balls(ball, count, 0, got[TO_X, here, :], gain[1:2], wqkv_t.at[1], h1, qkv1, p1, att1, inv1)
+        for nth in range(count):
+            arrive(TO_COT, ball + nth)
+        d_r = got[TO_COT, here, :]
+        d_att[:, here] = nt(wout[1], d_r).astype(BF16)
+        for nth in range(count):
+            backward_heads(ball + nth, nth, range(HEADS), d_att, qkv1, p1, att1, inv1, dqkv)
+        sent[BACK_D, here, :], gained = backward_norm(
+            ball, count, got[TO_X, here, :], gain[1:2], d_r, wqkv.at[1], dqkv
         )
-        arrive(TO_COT, ball)
-        d_r = got[TO_COT, cols(ball), :]
-        d_att[:, cols(ball)] = nt(wout[1], d_r).astype(BF16)
-        backward_heads(ball, 0, range(HEADS), d_att, qkv1, p1, att1, inv1, dqkv)
-        sent[BACK_D, cols(ball), :], gained = backward_norm(
-            ball, 1, got[TO_X, cols(ball), :], gain[1:2], d_r, wqkv.at[1], dqkv
-        )
-        send(BACK_D, ball)
+        for nth in range(count):
+            send(BACK_D, ball + nth)
         g_gain[1:2] += gained
 
     stores = []
@@ -527,15 +532,6 @@
         each.part[...] = nt(h1[...], dqkv[nth * half : (nth + 1) * half, :]).astype(BF16)
         advance(each)
 
-    @pl.loop(0, balls, step=PAIR)
-    def _(ball):
-        here = cols(ball, PAIR)
-        sent[BACK_R, here, :] = project(got[TO_X, here, :], att1[:, here], wout.at[1])
-        for nth in range(PAIR):
-            send(BACK_R, ball + nth)
-
-    sum_o.part[:, width:] = nn(att1[...], got[TO_COT]).astype(BF16)
-
     @pl.loop(0, balls)
     def _(ball):
         arrive(BACK_D, ball)
@@ -550,8 +546,6 @@
         def _():
             advance(*upper)
 
-    sum_o.part[:, :width] = nn(att0[...], y[...]).astype(BF16)
-    advance(sum_o)
     span_q = width // GROUPS
     heads = HEADS // GROUPS
     for group in range(GROUPS):
@@ -561,10 +555,6 @@
             backward_heads(
                 ball, ball, range(group * heads, (group + 1) * heads), d_att, qkv0, p0, att0, inv0, dqkv
             )
-
-            @pl.when(ball == 2)
-            def _():
-                advance(sum_o)
 
         for kind in range(3):
             low = kind * width + group * span_q
@@ -575,6 +565,17 @@
                 last[kind].part[...] = g
                 advance(last[kind])
         advance(*upper, sum_q)
+        if group == 0:
+            sum_o.part[:, :width] = nn(att0[...], y[...]).astype(BF16)
+            sum_o.part[:, width:] = nn(att1[...], got[TO_COT]).astype(BF16)
+        advance(sum_o)
+
+    @pl.loop(0, balls, step=PAIR)
+    def _(ball):
+        here = cols(ball, PAIR)
+        sent[BACK_R, here, :] = project(got[TO_X, here, :], att1[:, here], wout.at[1])
+        for nth in range(PAIR):
+            send(BACK_R, ball + nth)
 
     @pl.loop(0, balls, step=PAIR)
     def _(ball):
@@ -591,21 +592,6 @@
     small.send(g_gain[...])
     advance(*last, sum_q, *upper, sum_o)
     store(d_x, points_out.at[0])
-
-    @pl.loop(0, balls)
-    def _(ball):
-        arrive(BACK_R, ball)
-
-    @pl.loop(0, balls, step=PAIR)
-    def _(ball):
-        here = cols(ball, PAIR)
-        cot[here, :] = nn(one_hot_to_tree(order, ball * BALL, PAIR * BALL), got[BACK_R]).astype(BF16)
-
-        @pl.when(ball == 0)
-        def _():
-            advance(*last, sum_q, sum_o, *upper)
-
-    store(cot, mixed_out.at[0])
 
     def store_total(each):
         if each in upper:
@@ -621,6 +607,7 @@
             columns = pl.ds(last.index(each) * width + span_q, span_q)
             store(each.total, qkv_out.at[0, :, columns])
 
+    turn = 0
     while any(each.done < STEPS for each in sums):
         for each in (*last, sum_q, *upper, sum_o):
             if each.done < STEPS:
@@ -632,6 +619,15 @@
         elif small.done == 3:
             g_gain[...] = small.receive()
             store(g_gain.at[0:2], gain_out)
+        if turn in MIXED_TURNS:
+            ball = MIXED_TURNS.index(turn) * PAIR
+            if ball == 0:
+                for each in range(balls):
+                    arrive(BACK_R, each)
+            here = cols(ball, PAIR)
+            cot[here, :] = nn(one_hot_to_tree(order, ball * BALL, PAIR * BALL), got[BACK_R]).astype(BF16)
+            store(cot.at[here, :], mixed_out.at[0, here, :])
+        turn += 1
     for copy in stores:
         copy.wait()
     for each in sums:
@@ -710,7 +706,7 @@
             pltpu.VMEM((rows, rows), BF16),
             token,
             *saved(balls),
-            *saved(1),
+            *saved(balls - 2),
             pltpu.VMEM((3 * width, rows), BF16),
             pltpu.VMEM((width, rows), BF16),
             pltpu.VMEM((4, rows, width), BF16),

time: 107 us -> 109 us (1.019)
  Pallas kernels: 106 us -> 108 us
    pallas_call x1, Pallas kernels: 100 us -> 102 us  [local(): pl.pallas_call(kernel, out_shape=[jax.ShapeDtypeStruct(points.shape, BF16...]
where the time goes in v6:
time: 109 us
  Pallas kernels  108 us (99%)
    pallas_call x1, Pallas kernels, local(): pl.pallas_call(kernel, out_shape=[jax.ShapeDtypeStruct(points.shape, BF16...  102 us
    pallas_call x1, Pallas kernels, local(): pl.pallas_call(finish_kernel, out_shape=[jax.ShapeDtypeStruct(result.shap...  5.53 us

profile of v6, /device:TPU:1, one launch (start us, length us, event | category | flops | bytes accessed | tf_op | source)
XLA Modules:
  0.0 108.5 jit_solution(7280350432303539167)
XLA Ops:
  0.6 102.2 %shard_map.101 = (bf16[1,1024,512]{2,1,0:T(8,128)(2,1)}, bf16[1,1024,512]{2,1,0:T(8,128)(2,1)}, f32[2,512]{1,0:T(2,128)}, bf16[2,512,1536]{2,1,0:T(8,128)(2,1)}, bf16[2,512,512]{2,1,0:T(8,128)(2,1)}) custom-call(bf16[1,1024,512]{2,1,0:T(8,128)(2,1)} %points.1, s32[1,1024]{1,0:T(1,128)} %lists.1, f32[2,512]{1,0:T(2,128)} %gains.1, ...), custom_call_target="tpu_custom_call" | custom-call | tf_op jit(solution)/shard_map/pallas_call | solution.py:687
  102.8 5.5 %shard_map.102 = (bf16[1,1024,512]{2,1,0:T(8,128)(2,1)}, bf16[1,1024,512]{2,1,0:T(8,128)(2,1)}, f32[2,512]{1,0:T(2,128)}, f32[2,512,1536]{2,1,0:T(8,128)}, f32[2,512,512]{2,1,0:T(8,128)}) custom-call(bf16[1,1024,512]{2,1,0:T(8,128)(2,1)} %get-tuple-element.10.mixed, bf16[1,1024,512]{2,1,0:T(8,128)(2,1)} %get-tuple-element.11.d_x, ...), custom_call_target="tpu_custom_call" | custom-call | tf_op jit(solution)/shard_map/pallas_call | solution.py:733

commit v7 on v4

--- a/solution.py
+++ b/solution.py
@@ -56,8 +56,10 @@
     unit = jnp.where(
         lax.broadcasted_iota(jnp.int32, (BALL, BALL), 0) == lax.broadcasted_iota(jnp.int32, (BALL, BALL), 1), 1.0, 0.0
     ).astype(BF16)
-    for low in range(0, wqkv.shape[1], BALL):
-        wqkv_t[low : low + BALL, :] = nt(unit, wqkv[:, low : low + BALL]).astype(BF16)
+
+    @pl.loop(0, wqkv.shape[1] // BALL)
+    def _(tile):
+        wqkv_t[cols(tile), :] = nt(unit, wqkv[:, cols(tile)]).astype(BF16)
 
 
 def forward_balls(ball, count, keep, x, gain, wqkv_t, wout, h_t, qkv_t, p_t, att_t, inv):
@@ -72,9 +74,8 @@
 
     def score(item):
         nth, head = item
-        low = head * size
-        q = qkv_t[low : low + size, cols(ball + nth)] * size ** (-0.5)
-        return tn(qkv_t[width + low : width + low + size, cols(ball + nth)], q)
+        q = qkv_t[rows_of(head, 0, width), cols(ball + nth)] * size ** (-0.5)
+        return tn(qkv_t[rows_of(head, 1, width), cols(ball + nth)], q)
 
     def weigh(item, scores):
         nth, head = item
@@ -82,17 +83,24 @@
         share = 1.0 / jnp.sum(weights, axis=0, keepdims=True)
         weights = weights.astype(BF16)
         p_t[keep + nth, head] = weights
-        inv[keep + nth, head : head + 1, :] = share
+        inv[keep + nth, pl.ds(head, 1), :] = share
         return weights, share
 
     def mix(item, weights, share):
         nth, head = item
-        low = head * size
-        v = qkv_t[2 * width + low : 2 * width + low + size, cols(ball + nth)]
-        att_t[low : low + size, cols(ball + nth)] = (nn(v, weights) * share).astype(BF16)
-
-    staggered([(nth, head) for nth in range(count) for head in range(HEADS)], score, weigh, mix)
+        v = qkv_t[rows_of(head, 2, width), cols(ball + nth)]
+        att_t[rows_of(head, 0, width), cols(ball + nth)] = (nn(v, weights) * share).astype(BF16)
+
+    @pl.loop(0, count * HEADS, step=ROLL)
+    def _(first):
+        staggered([(first // HEADS, first % HEADS + each) for each in range(ROLL)], score, weigh, mix)
+
     return values + tn(att_t[:, here], wout[...])
+
+
+def rows_of(head, part, width):
+    size = width // HEADS
+    return pl.ds(pl.multiple_of(part * width + head * size, size), size)
 
 
 def staggered(heads, *stages):
@@ -101,10 +109,9 @@
     for step in range(len(heads) + len(stages) - 1):
         for index, stage in enumerate(stages):
             if 0 <= step - index < len(heads):
-                head = heads[step - index]
-                given = held.pop((head, index), ())
-                result = stage(head, *given)
-                held[head, index + 1] = result if isinstance(result, tuple) else (result,)
+                given = held.pop((step - index, index), ())
+                result = stage(heads[step - index], *given)
+                held[step - index, index + 1] = result if isinstance(result, tuple) else (result,)
 
 
 def backward_heads(ball, keep, heads, d_att, qkv_t, p_t, att_t, inv, dqkv_t):
@@ -113,26 +120,26 @@
     here = cols(ball)
 
     def weigh(head):
-        low = head * size
-        v = qkv_t[2 * width + low : 2 * width + low + size, here]
-        d_out = d_att[low : low + size, here].astype(F32) * inv[keep, head : head + 1, :]
-        delta = jnp.sum(d_out * att_t[low : low + size, here].astype(F32), axis=0, keepdims=True)
+        rows = rows_of(head, 0, width)
+        d_out = d_att[rows, here].astype(F32) * inv[keep, pl.ds(head, 1), :]
+        delta = jnp.sum(d_out * att_t[rows, here].astype(F32), axis=0, keepdims=True)
         d_out = d_out.astype(BF16)
-        return d_out, delta, tn(v, d_out)
+        return d_out, delta, tn(qkv_t[rows_of(head, 2, width), here], d_out)
 
     def score(head, d_out, delta, d_weights):
         weights = p_t[keep, head]
         return d_out, weights, (weights.astype(F32) * (d_weights - delta)).astype(BF16)
 
     def spread(head, d_out, weights, d_scores):
-        low = head * size
-        q = qkv_t[low : low + size, here] * size ** (-0.5)
-        k = qkv_t[width + low : width + low + size, here]
-        dqkv_t[low : low + size, here] = (nn(k, d_scores) * size ** (-0.5)).astype(BF16)
-        dqkv_t[width + low : width + low + size, here] = nt(q, d_scores).astype(BF16)
-        dqkv_t[2 * width + low : 2 * width + low + size, here] = nt(d_out, weights).astype(BF16)
-
-    staggered(heads, weigh, score, spread)
+        q = qkv_t[rows_of(head, 0, width), here] * size ** (-0.5)
+        k = qkv_t[rows_of(head, 1, width), here]
+        dqkv_t[rows_of(head, 0, width), here] = (nn(k, d_scores) * size ** (-0.5)).astype(BF16)
+        dqkv_t[rows_of(head, 1, width), here] = nt(q, d_scores).astype(BF16)
+        dqkv_t[rows_of(head, 2, width), here] = nt(d_out, weights).astype(BF16)
+
+    @pl.loop(heads.start, heads.stop, step=ROLL)
+    def _(first):
+        staggered([first + each for each in range(ROLL)], weigh, score, spread)
 
 
 def backward_norm(ball, count, x, gain, dy, wqkv, dqkv_t):
@@ -272,7 +279,14 @@
             self.partner(HALVES).start()
         elif step == 1:
             self.arrive(HALVES)
-            self.part[self.span(1), :] = self.add(self.span(1), everything, self.halves[...])
+            base = self.bases[1]
+
+            @pl.loop(0, self.sizes[1] // 32)
+            def _(tile):
+                rows = pl.ds(pl.multiple_of(base + tile * 32, 32), 32)
+                held = pl.ds(pl.multiple_of(tile * 32, 32), 32)
+                self.part[rows, :] = self.add(rows, everything, self.halves[held, :])
+
             self.start_around(TURN)
         elif step == 2:
             self.arrive(TURN)
@@ -362,6 +376,7 @@
 TO_X, TO_COT, BACK_R, BACK_D = range(4)
 GROUPS = 2
 PAIR = 2
+ROLL = 4
 SUMS = (
     (1024, ("x", "z", "y")),
     (1024, ("z", "x", "y")),
@@ -522,9 +537,16 @@
 
     width = x.shape[1]
     first, second = upper[0].part, upper[1].part
+
+    @pl.loop(0, 2 * width // BALL)
+    def _(tile):
+        first[:, cols(tile)] = nt(h1[...], dqkv[cols(tile), :]).astype(BF16)
+
+    @pl.loop(0, width // BALL)
+    def _(tile):
+        second[:, cols(tile)] = nt(h1[...], dqkv[cols(2 * width // BALL + tile), :]).astype(BF16)
+
     second[:, width:] = nn(att1[...], got[TO_COT]).astype(BF16)
-    first[...] = nt(h1[...], dqkv[: 2 * width, :]).astype(BF16)
-    second[:, :width] = nt(h1[...], dqkv[2 * width :, :]).astype(BF16)
 
     def advance(*which):
         for each in which:
@@ -562,13 +584,17 @@
             def _():
                 advance(sum_o)
 
-        for kind in range(3):
-            low = kind * width + group * span_q
-            g = nt(h0[...], dqkv[low : low + span_q, :]).astype(BF16)
-            if group == 0:
-                sum_q.part[:, kind * span_q : (kind + 1) * span_q] = g
-            else:
-                last[kind].part[...] = g
+        if group == 0:
+
+            @pl.loop(0, 3)
+            def _(kind):
+                rows = cols(kind * (width // BALL))
+                sum_q.part[:, cols(kind)] = nt(h0[...], dqkv[rows, :]).astype(BF16)
+
+        else:
+            for kind in range(3):
+                rows = cols(kind * (width // BALL) + 1)
+                last[kind].part[...] = nt(h0[...], dqkv[rows, :]).astype(BF16)
                 advance(last[kind])
         advance(*upper, sum_q)
 

time: 106 us -> 111 us (1.047)
  Pallas kernels: 106 us -> 110 us
    pallas_call x1, Pallas kernels: 100 us -> 104 us  [local(): pl.pallas_call(kernel, out_shape=[jax.ShapeDtypeStruct(points.shape, BF16...]
where the time goes in v7:
time: 111 us
  Pallas kernels  110 us (99%)
    pallas_call x1, Pallas kernels, local(): pl.pallas_call(kernel, out_shape=[jax.ShapeDtypeStruct(points.shape, BF16...  104 us
    pallas_call x1, Pallas kernels, local(): pl.pallas_call(finish_kernel, out_shape=[jax.ShapeDtypeStruct(result.shap...  5.53 us

profile of v7, /device:TPU:1, one launch (start us, length us, event | category | flops | bytes accessed | tf_op | source)
XLA Modules:
  0.0 110.7 jit_solution(13905645055775475737)
XLA Ops:
  0.6 104.4 %shard_map.101 = (bf16[1,1024,512]{2,1,0:T(8,128)(2,1)}, bf16[1,1024,512]{2,1,0:T(8,128)(2,1)}, f32[2,512]{1,0:T(2,128)}, bf16[2,512,1536]{2,1,0:T(8,128)(2,1)}, bf16[2,512,512]{2,1,0:T(8,128)(2,1)}) custom-call(bf16[1,1024,512]{2,1,0:T(8,128)(2,1)} %points.1, s32[1,1024]{1,0:T(1,128)} %lists.1, f32[2,512]{1,0:T(2,128)} %gains.1, ...), custom_call_target="tpu_custom_call" | custom-call | tf_op jit(solution)/shard_map/pallas_call | solution.py:715
  105.0 5.5 %shard_map.102 = (bf16[1,1024,512]{2,1,0:T(8,128)(2,1)}, bf16[1,1024,512]{2,1,0:T(8,128)(2,1)}, f32[2,512]{1,0:T(2,128)}, f32[2,512,1536]{2,1,0:T(8,128)}, f32[2,512,512]{2,1,0:T(8,128)}) custom-call(bf16[1,1024,512]{2,1,0:T(8,128)(2,1)} %get-tuple-element.10.mixed, bf16[1,1024,512]{2,1,0:T(8,128)(2,1)} %get-tuple-element.11.d_x, ...), custom_call_target="tpu_custom_call" | custom-call | tf_op jit(solution)/shard_map/pallas_call | solution.py:761

commit v8 on v4

--- a/solution.py
+++ b/solution.py
@@ -491,21 +491,24 @@
     transpose_by_unit(wqkv.at[1], wqkv_t.at[1])
     g_gain[...] = jnp.zeros_like(g_gain)
 
-    @pl.loop(0, balls)
-    def _(ball):
-        arrive(TO_X, ball)
-        rows_x = got[TO_X, cols(ball), :]
-        sent[BACK_R, cols(ball), :] = forward_balls(
-            ball, 1, 0, rows_x, gain[1:2], wqkv_t.at[1], wout.at[1], h1, qkv1, p1, att1, inv1
+    for ball, count in ((0, 1), (1, balls - 2), (balls - 1, 1)):
+        here = cols(ball, count)
+        for nth in range(count):
+            arrive(TO_X, ball + nth)
+        sent[BACK_R, here, :] = forward_balls(
+            ball, count, 0, got[TO_X, here, :], gain[1:2], wqkv_t.at[1], wout.at[1], h1, qkv1, p1, att1, inv1
         ).astype(BF16)
-        arrive(TO_COT, ball)
-        d_r = got[TO_COT, cols(ball), :]
-        d_att[:, cols(ball)] = nt(wout[1], d_r).astype(BF16)
-        backward_heads(ball, 0, range(HEADS), d_att, qkv1, p1, att1, inv1, dqkv)
-        sent[BACK_D, cols(ball), :], gained = backward_norm(
-            ball, 1, got[TO_X, cols(ball), :], gain[1:2], d_r, wqkv.at[1], dqkv
+        for nth in range(count):
+            arrive(TO_COT, ball + nth)
+        d_r = got[TO_COT, here, :]
+        d_att[:, here] = nt(wout[1], d_r).astype(BF16)
+        for nth in range(count):
+            backward_heads(ball + nth, nth, range(HEADS), d_att, qkv1, p1, att1, inv1, dqkv)
+        sent[BACK_D, here, :], gained = backward_norm(
+            ball, count, got[TO_X, here, :], gain[1:2], d_r, wqkv.at[1], dqkv
         )
-        send(BACK_D, ball)
+        for nth in range(count):
+            send(BACK_D, ball + nth)
         g_gain[1:2] += gained
 
     @pl.loop(0, balls)
@@ -708,7 +711,7 @@
             pltpu.VMEM((rows, rows), BF16),
             token,
             *saved(balls),
-            *saved(1),
+            *saved(balls - 2),
             pltpu.VMEM((3 * width, rows), BF16),
             pltpu.VMEM((width, rows), BF16),
             pltpu.VMEM((4, rows, width), BF16),

time: 106 us -> 106 us (level)
  no operation moved by 1% of the time
where the time goes in v8:
time: 106 us
  Pallas kernels  106 us (100%)
    pallas_call x1, Pallas kernels, local(): pl.pallas_call(kernel, out_shape=[jax.ShapeDtypeStruct(points.shape, BF16...  100 us
    pallas_call x1, Pallas kernels, local(): pl.pallas_call(finish_kernel, out_shape=[jax.ShapeDtypeStruct(result.shap...  5.53 us

profile of v8, /device:TPU:1, one launch (start us, length us, event | category | flops | bytes accessed | tf_op | source)
XLA Modules:
  0.0 106.3 jit_solution(5241583818118102163)
XLA Ops:
  0.6 100.0 %shard_map.101 = (bf16[1,1024,512]{2,1,0:T(8,128)(2,1)}, bf16[1,1024,512]{2,1,0:T(8,128)(2,1)}, f32[2,512]{1,0:T(2,128)}, bf16[2,512,1536]{2,1,0:T(8,128)(2,1)}, bf16[2,512,512]{2,1,0:T(8,128)(2,1)}) custom-call(bf16[1,1024,512]{2,1,0:T(8,128)(2,1)} %points.1, s32[1,1024]{1,0:T(1,128)} %lists.1, f32[2,512]{1,0:T(2,128)} %gains.1, ...), custom_call_target="tpu_custom_call" | custom-call | tf_op jit(solution)/shard_map/pallas_call | solution.py:692
  100.6 5.5 %shard_map.102 = (bf16[1,1024,512]{2,1,0:T(8,128)(2,1)}, bf16[1,1024,512]{2,1,0:T(8,128)(2,1)}, f32[2,512]{1,0:T(2,128)}, f32[2,512,1536]{2,1,0:T(8,128)}, f32[2,512,512]{2,1,0:T(8,128)}) custom-call(bf16[1,1024,512]{2,1,0:T(8,128)(2,1)} %get-tuple-element.10.mixed, bf16[1,1024,512]{2,1,0:T(8,128)(2,1)} %get-tuple-element.11.d_x, ...), custom_call_target="tpu_custom_call" | custom-call | tf_op jit(solution)/shard_map/pallas_call | solution.py:738
